TPU v7x, 32 devices: a whole 2x2x4 slice. The times are simulated.
32 devices in a mesh: res: 8 (over z, y), head: 4 (over x, core).
Axes of the slice: x: 2, y: 2, z: 4, core: 2. Of those that a mesh axis runs over, the one named last changes fastest.
Arguments:
- pair_input: bfloat16 [2, 256, 256, 128], P(None, 'res'), may hold values from -6 to 6
- lengths: int32 [2], replicated, may hold values from 60 to 256, as said below
- distogram_bins: int32 [2, 256, 256], P(None, 'res'), may hold values from 0 to 63
- head_proj: float32 [128, 512], P(None, 'head'), may hold values from -0.5 to 0.5
- bias_proj: float32 [128, 4], P(None, 'head'), may hold values from -0.5 to 0.5
- output_proj: float32 [128, 128], P('head'), may hold values from -4 to 4
- expand_proj: float32 [128, 512], P(None, 'head'), may hold values from -0.5 to 0.5
- reduce_proj: float32 [512, 128], P('head'), may hold values from -0.25 to 0.25
- distogram_proj: float32 [128, 64], replicated, may hold values from -0.5 to 0.5
- small_params: float32 [320], replicated, may hold values from 0.5 to 1.5
- momentum_head: float32 [128, 512], P(None, 'head'), may hold values from -2e-05 to 2e-05
- momentum_bias: float32 [128, 4], P(None, 'head'), may hold values from -2e-05 to 2e-05
- momentum_output: float32 [128, 128], P('head'), may hold values from -2e-05 to 2e-05
- momentum_expand: float32 [128, 512], P(None, 'head'), may hold values from -2e-05 to 2e-05
- momentum_reduce: float32 [512, 128], P('head'), may hold values from -2e-05 to 2e-05
- momentum_distogram: float32 [128, 64], replicated, may hold values from -2e-05 to 2e-05
- momentum_small: float32 [320], replicated, may hold values from -5e-05 to 5e-05
- average_head: float32 [128, 512], P(None, 'head'), may hold values from -0.5 to 0.5
- average_bias: float32 [128, 4], P(None, 'head'), may hold values from -0.5 to 0.5
- average_output: float32 [128, 128], P('head'), may hold values from -4 to 4
- average_expand: float32 [128, 512], P(None, 'head'), may hold values from -0.5 to 0.5
- average_reduce: float32 [512, 128], P('head'), may hold values from -0.25 to 0.25
- average_distogram: float32 [128, 64], replicated, may hold values from -0.5 to 0.5
- average_small: float32 [320], replicated, may hold values from 0.5 to 1.5
Outputs:
- total_loss: float32 [], replicated
- gradient_norm: float32 [], replicated
- head_weight: float32 [128, 512], P(None, 'head')
- bias_weight: float32 [128, 4], P(None, 'head')
- output_weight: float32 [128, 128], P('head')
- expand_weight: float32 [128, 512], P(None, 'head')
- reduce_weight: float32 [512, 128], P('head')
- distogram_weight: float32 [128, 64], replicated
- small_weight: float32 [320], replicated
- head_velocity: float32 [128, 512], P(None, 'head')
- bias_velocity: float32 [128, 4], P(None, 'head')
- output_velocity: float32 [128, 128], P('head')
- expand_velocity: float32 [128, 512], P(None, 'head')
- reduce_velocity: float32 [512, 128], P('head')
- distogram_velocity: float32 [128, 64], replicated
- small_velocity: float32 [320], replicated
- head_average: float32 [128, 512], P(None, 'head')
- bias_average: float32 [128, 4], P(None, 'head')
- output_average: float32 [128, 128], P('head')
- expand_average: float32 [128, 512], P(None, 'head')
- reduce_average: float32 [512, 128], P('head')
- distogram_average: float32 [128, 64], replicated
- small_average: float32 [320], replicated
Inputs may be any that keep to these rules, and one draw needn't show every extreme that they name: `lengths`: item 0 has length 256; the others lie between min(60, 256) and 256.
All inputs are finite; a program needn't handle non-finite values.
Results may differ from a plain program's by a relative error of at most 0.0085.
Values may be sent and summed in bfloat16 or wider, within the bound.
A program may use at most 192 MiB of HBM per device.

v0:
```python
from functools import partial

import jax
import jax.numpy as jnp
from jax import lax
from jax.experimental import pallas as pl
from jax.experimental.pallas import tpu as pltpu
from jax.sharding import PartitionSpec as P

EPS = 1e-05
NEG = -1000000000.0
MOMENTUM = 0.9
RATE = 20000.0
KEEP = 0.9
CLIP = 0.002


def project(values, weight):
    return jnp.einsum("rjc,cd->rjd", values, weight, preferred_element_type=jnp.float32)


def layer_norm(values, gain):
    center = values - jnp.mean(values, -1, keepdims=True)
    spread = jnp.mean(center * center, -1, keepdims=True)
    return center * lax.rsqrt(spread + EPS) * gain


def norm_back(values, gain, grad_out):
    result, pull = jax.vjp(layer_norm, values, gain)
    return pull(grad_out)


def row_scores(query, key, bias_full, penalty, scale):
    scores = jnp.dot(query, key.T, preferred_element_type=jnp.float32) * scale
    return scores + bias_full.astype(jnp.float32) + penalty[None, :]


def forward_row(bias_full, penalty, scale, row):
    query, key, value, gate = row
    scores = row_scores(query, key, bias_full, penalty, scale)
    peak = jnp.max(scores, -1, keepdims=True)
    expo = jnp.exp(scores - peak)
    summed = jnp.sum(expo, -1, keepdims=True)
    probs = (expo / summed).astype(jnp.bfloat16)
    mixed = jnp.dot(probs, value, preferred_element_type=jnp.float32)
    gated = (mixed * jax.nn.sigmoid(gate)).astype(jnp.bfloat16)
    return (gated, (peak + jnp.log(summed))[:, 0])


def backward_row(bias_full, penalty, scale, carry, row):
    query, key, value, gate, dgated, logsum = row
    scores = row_scores(query, key, bias_full, penalty, scale)
    exact = jnp.exp(scores - logsum[:, None])
    probs = exact.astype(jnp.bfloat16)
    mixed = jnp.dot(probs, value, preferred_element_type=jnp.float32)
    sigma = jax.nn.sigmoid(gate)
    dmixed = (dgated * sigma).astype(jnp.bfloat16)
    dgate = dgated * mixed * sigma * (1.0 - sigma)
    dvalue = jnp.dot(probs.T, dmixed, preferred_element_type=jnp.float32)
    dprobs = jnp.dot(dmixed, value.T, preferred_element_type=jnp.float32)
    inner = jnp.sum(dprobs * exact, -1, keepdims=True)
    dscores = (exact * (dprobs - inner)).astype(jnp.bfloat16)
    dquery = jnp.dot(dscores, key, preferred_element_type=jnp.float32) * scale
    dkey = jnp.dot(dscores.T, query, preferred_element_type=jnp.float32) * scale
    grads = jnp.concatenate([dquery, dkey, dvalue, dgate], -1)
    return (carry + dscores.astype(jnp.float32), grads)


def advance(weight, moment, average, grad):
    velocity = MOMENTUM * moment + grad
    fresh = weight - RATE * (grad + MOMENTUM * velocity)
    return (fresh, velocity, KEEP * average + (1.0 - KEEP) * fresh)


def general_body(
    pair_input,
    lengths,
    distogram_bins,
    head_proj,
    bias_proj,
    output_proj,
    expand_proj,
    reduce_proj,
    distogram_proj,
    small_params,
    momentum_head,
    momentum_bias,
    momentum_output,
    momentum_expand,
    momentum_reduce,
    momentum_distogram,
    momentum_small,
    average_head,
    average_bias,
    average_output,
    average_expand,
    average_reduce,
    average_distogram,
    average_small,
):
    weights = (
        head_proj,
        bias_proj,
        output_proj,
        expand_proj,
        reduce_proj,
        distogram_proj,
        small_params,
    )
    momenta = (
        momentum_head,
        momentum_bias,
        momentum_output,
        momentum_expand,
        momentum_reduce,
        momentum_distogram,
        momentum_small,
    )
    averages = (
        average_head,
        average_bias,
        average_output,
        average_expand,
        average_reduce,
        average_distogram,
        average_small,
    )
    head_w, bias_w, out_w, expand_w, reduce_w, dist_w = [
        w.astype(jnp.bfloat16) for w in weights[:6]
    ]
    items, rows, length, channels = pair_input.shape
    width = output_proj.shape[0]
    scale = width ** (-0.5)
    gain_one = small_params[:channels]
    gain_two = small_params[channels : 2 * channels]
    dist_bias = small_params[2 * channels :]
    positions = jnp.arange(length)
    first_row = lax.axis_index("res") * rows
    size_f = lengths.astype(jnp.float32)
    count = jnp.sum(size_f * size_f)
    grads = [jnp.zeros_like(w) for w in weights]
    loss_part = jnp.zeros((), jnp.float32)
    for item in range(items):
        live = (positions < lengths[item]).astype(jnp.float32)
        penalty = (1.0 - live) * NEG
        row_live = lax.dynamic_slice_in_dim(live, first_row, rows)
        start = pair_input[item].astype(jnp.float32)
        normed = layer_norm(start, gain_one).astype(jnp.bfloat16)
        proj = project(normed, head_w)
        query = proj[..., :width].astype(jnp.bfloat16)
        key = proj[..., width : 2 * width].astype(jnp.bfloat16)
        value = proj[..., 2 * width : 3 * width].astype(jnp.bfloat16)
        gate = proj[..., 3 * width :]
        bias_local = project(normed, bias_w)[..., 0].astype(jnp.bfloat16)
        bias_full = lax.all_gather(bias_local, "res", axis=0, tiled=True)
        gated, logsum = lax.map(
            partial(forward_row, bias_full, penalty, scale), (query, key, value, gate)
        )
        first = start + lax.psum(project(gated, out_w), "head")
        widened = layer_norm(first, gain_two).astype(jnp.bfloat16)
        pre = project(widened, expand_w)
        hidden = jnp.maximum(pre, 0.0).astype(jnp.bfloat16)
        second = first + lax.psum(project(hidden, reduce_w).astype(jnp.bfloat16), "head").astype(
            jnp.float32
        )
        second_low = second.astype(jnp.bfloat16)
        half = project(second_low, dist_w)
        mirror = lax.all_to_all(
            half.astype(jnp.bfloat16), "res", split_axis=1, concat_axis=0, tiled=True
        ).astype(half.dtype)
        logits = half + jnp.transpose(mirror, (1, 0, 2)) + dist_bias
        peak = jnp.max(logits, -1, keepdims=True)
        logp = logits - peak - jnp.log(jnp.sum(jnp.exp(logits - peak), -1, keepdims=True))
        onehot = (distogram_bins[item][:, :, None] == jnp.arange(logits.shape[2])).astype(
            jnp.float32
        )
        weight = (row_live[:, None] * live[None, :])[:, :, None]
        loss_part = loss_part - jnp.sum(logp * onehot * weight) / count
        dlogits = (jnp.exp(logp) - onehot) * weight / count
        back = lax.all_to_all(
            dlogits.astype(jnp.bfloat16), "res", split_axis=1, concat_axis=0, tiled=True
        ).astype(dlogits.dtype)
        dhalf = (dlogits + jnp.transpose(back, (1, 0, 2))).astype(jnp.bfloat16)
        grads[5] = grads[5] + jnp.einsum(
            "rjc,rjb->cb", second_low, dhalf, preferred_element_type=jnp.float32
        )
        dist_grad = jnp.sum(dlogits, (0, 1))
        dsecond = jnp.einsum("rjb,cb->rjc", dhalf, dist_w, preferred_element_type=jnp.float32)
        dtrans = dsecond.astype(jnp.bfloat16)
        grads[4] = grads[4] + jnp.einsum(
            "rjh,rjc->hc", hidden, dtrans, preferred_element_type=jnp.float32
        )
        dhidden = jnp.einsum("rjc,hc->rjh", dtrans, reduce_w, preferred_element_type=jnp.float32)
        dpre = jnp.where(pre > 0, dhidden, 0.0).astype(jnp.bfloat16)
        grads[3] = grads[3] + jnp.einsum(
            "rjc,rjh->ch", widened, dpre, preferred_element_type=jnp.float32
        )
        dwidened = lax.psum(
            jnp.einsum("rjh,ch->rjc", dpre, expand_w, preferred_element_type=jnp.float32).astype(
                jnp.bfloat16
            ),
            "head",
        ).astype(jnp.float32)
        dfirst_norm, gain_two_grad = norm_back(first, gain_two, dwidened)
        dout = (dsecond + dfirst_norm).astype(jnp.bfloat16)
        grads[2] = grads[2] + jnp.einsum(
            "rjd,rjc->dc", gated, dout, preferred_element_type=jnp.float32
        )
        dgated = jnp.einsum("rjc,dc->rjd", dout, out_w, preferred_element_type=jnp.float32)
        bias_terms, dproj = lax.scan(
            partial(backward_row, bias_full, penalty, scale),
            jnp.zeros((length, length), jnp.float32),
            (query, key, value, gate, dgated, logsum),
        )
        dproj = dproj.astype(jnp.bfloat16)
        dbias = lax.psum_scatter(bias_terms, "res", scatter_dimension=0, tiled=True).astype(
            jnp.bfloat16
        )
        grads[0] = grads[0] + jnp.einsum(
            "rjc,rjd->cd", normed, dproj, preferred_element_type=jnp.float32
        )
        grads[1] = (
            grads[1]
            + jnp.einsum("rjc,rj->c", normed, dbias, preferred_element_type=jnp.float32)[:, None]
        )
        dnormed_part = jnp.einsum("rjd,cd->rjc", dproj, head_w, preferred_element_type=jnp.float32)
        dnormed_part = dnormed_part + dbias.astype(jnp.float32)[:, :, None] * bias_w[:, 0].astype(
            jnp.float32
        )
        dnormed = lax.psum(dnormed_part.astype(jnp.bfloat16), "head").astype(jnp.float32)
        unused, gain_one_grad = norm_back(start, gain_one, dnormed)
        grads[6] = grads[6] + jnp.concatenate([gain_one_grad, gain_two_grad, dist_grad])
    summed = lax.psum(
        (grads[0], grads[1], grads[2], grads[3], grads[4], grads[5], grads[6], loss_part), "res"
    )
    total_grads = summed[:7]
    total_loss = summed[7]
    owned = jnp.zeros((), jnp.float32)
    for grad in total_grads[:5]:
        owned = owned + jnp.sum(grad * grad)
    shared = jnp.sum(total_grads[5] * total_grads[5]) + jnp.sum(total_grads[6] * total_grads[6])
    grad_norm = jnp.sqrt(shared + lax.psum(owned, "head"))
    factor = CLIP / jnp.maximum(grad_norm, CLIP)
    results = [
        advance(w, m, a, g * factor) for w, m, a, g in zip(weights, momenta, averages, total_grads)
    ]
    new_w = [r[0] for r in results]
    new_m = [r[1] for r in results]
    new_a = [r[2] for r in results]
    return (
        total_loss,
        grad_norm,
        new_w[0],
        new_w[1],
        new_w[2],
        new_w[3],
        new_w[4],
        new_w[5],
        new_w[6],
        new_m[0],
        new_m[1],
        new_m[2],
        new_m[3],
        new_m[4],
        new_m[5],
        new_m[6],
        new_a[0],
        new_a[1],
        new_a[2],
        new_a[3],
        new_a[4],
        new_a[5],
        new_a[6],
    )


NT = (((1,), (1,)), ((), ()))
NN = (((1,), (0,)), ((), ()))
F32 = jnp.float32
LOW = jnp.bfloat16
LOG2E = 1.4426950408889634


def dot(left, right, dims=NN):
    return lax.dot_general(left, right, dims, preferred_element_type=F32)


def iota(shape, dim):
    return lax.broadcasted_iota(jnp.int32, shape, dim)


def eye(size):
    return (iota((size, size), 0) == iota((size, size), 1)).astype(F32).astype(LOW)


def sigmoid(x):
    return 0.5 * jnp.tanh(0.5 * x) + 0.5


def step_kernel(groups, heads, *refs):
    (
        pair, lengths, bins, head_w, bias_w, out_w, exp_w, red_w, dist_w, small,
        o_head, o_block, o_dist, o_small,
        normed, tok, qkv, sig, expo, mixed, rinv,
        wc, wt, we, wet, wr, wrt, wo, wot, wd, wdt, gain_col, dist_col,
        bias_f, bias_send, bias_all, bias_t, bins_low, bins_in, bins_own, bins_t,
        gated, gall, xhat, rstd, widened, hidden, slow, halves, pack_f, half_send, half_in, mirror,
        dpre_s, dg_send, dg_in, g_out, g_red, g_exp, g_dist, loss_acc, dist_acc,
        block_send, block_in, block_sum,
        db_acc, db_send, db_in, g_head, g_bias, head_in, head_sum, small_own, small_in, card, card_in,
        sem_bias_s, sem_bias_r, sem_bins_s, sem_bins_r, sem_w_s, sem_w_r,
        sem_gat_s, sem_gat_r, sem_half_s, sem_half_r, sem_dg_s, sem_dg_r,
        sem_blk_s, sem_blk_r, sem_gath_s, sem_gath_r, sem_db_s, sem_db_r,
        sem_head_s, sem_head_r, sem_small_s, sem_small_r, sem_card_s, sem_card_r, sem_fin_s, sem_fin_r,
    ) = refs
    items, rows, length, chan = pair.shape
    width = out_w.shape[0]
    nbins = dist_w.shape[1]
    unit = exp_w.shape[1]
    own = rows // heads
    half_own = own // 2
    total = groups * heads
    scale = width ** (-0.5)
    my_r = lax.axis_index("res")
    my_h = lax.axis_index("head")
    me = my_r * heads + my_h

    def device(r, h):
        return {"res": r, "head": h}

    def send(src, dst, ssem, rsem, r, h):
        return pltpu.make_async_remote_copy(
            src_ref=src, dst_ref=dst, send_sem=ssem, recv_sem=rsem,
            device_id=device(r, h), device_id_type=pl.DeviceIdType.MESH,
        )

    def res_peer(o):
        return lax.rem(my_r + o, groups)

    def head_peer(o):
        return lax.rem(my_h + o, heads)

    def any_peer(o):
        d = lax.rem(me + o, total)
        return d, d // heads, lax.rem(d, heads)

    def each(count, make, act):
        def one(o, carry):
            act(make(o))
            return carry
        lax.fori_loop(1, count, one, 0)

    start = lambda c: c.start()
    wait_in = lambda c: c.wait_recv()
    wait_out = lambda c: c.wait_send()

    barrier = pltpu.get_barrier_semaphore()

    def greet(o, carry):
        d, r, h = any_peer(o)
        pl.semaphore_signal(barrier, inc=1, device_id=device(r, h), device_id_type=pl.DeviceIdType.MESH)
        return carry

    lax.fori_loop(1, total, greet, 0)

    hw = head_w[...]
    hw_low = hw.astype(LOW)
    wc[0 : 4 * width] = jnp.transpose(hw).astype(LOW)
    brow = bias_w[...].astype(LOW).astype(F32)
    wc[4 * width :] = jnp.where(iota((16, chan), 0) == 0, brow, 0.0).astype(LOW)
    src_col = iota((4 * width, 4 * width), 0)
    dst_col = iota((4 * width, 4 * width), 1)
    want = jnp.where(
        dst_col < width, dst_col + width, jnp.where(dst_col < 3 * width, dst_col, -1)
    )
    wt[...] = dot(hw_low, (src_col == want).astype(F32).astype(LOW)).astype(LOW)
    ident = eye(chan)
    ident_l = eye(length)
    gain_one = small[:, 0:chan]
    gain_two = small[:, chan : 2 * chan]
    gain_col[...] = jnp.transpose(jnp.broadcast_to(gain_two, (chan, chan)))
    dist_col[...] = jnp.transpose(jnp.broadcast_to(small[:, 2 * chan : 3 * chan], (chan, chan)))[:nbins]
    we[:, pl.ds(pl.multiple_of(my_h * unit, unit), unit)] = exp_w[...].astype(LOW)
    wr[pl.ds(pl.multiple_of(my_h * unit, unit), unit), :] = red_w[...].astype(LOW)
    wo[pl.ds(pl.multiple_of(my_h * width, width), width), :] = out_w[...].astype(LOW)
    wd[...] = dist_w[...].astype(LOW)
    wdt[...] = dot(eye(nbins), wd[...], NT).astype(LOW)
    bins_low[...] = bins[...].astype(F32).astype(LOW)
    bins_own[...] = bins[:, pl.ds(pl.multiple_of(my_h * own, own), own), :].astype(F32)
    one_lane = (iota((1, 4 * width), 1) >= 3 * width).astype(F32)

    def before(item):
        def row(r, carry):
            x = pair[item, r].astype(F32)
            center = x - jnp.mean(x, -1, keepdims=True)
            spread = jnp.mean(center * center, -1, keepdims=True)
            low = (center * lax.rsqrt(spread + EPS) * gain_one).astype(LOW)
            normed[item, r] = low
            ch = dot(wc[...], low, NT)
            qkv[item, r] = ch[: 3 * width].astype(LOW)
            sig[item, r] = sigmoid(ch[3 * width : 4 * width])
            bias_f[pl.ds(r, 1), :] = ch[4 * width : 4 * width + 1]
            tok[item, r] = (dot(low, wt[...]) + one_lane).astype(LOW)
            return carry
        lax.fori_loop(0, rows, row, 0, unroll=2)
        bias_send[item] = bias_f[...].astype(LOW)
        bias_all[item, pl.ds(pl.multiple_of(my_r * rows, rows), rows), :] = bias_f[...].astype(LOW)

    def bias_copy(item):
        def make(o):
            return send(
                bias_send.at[item],
                bias_all.at[item, pl.ds(pl.multiple_of(my_r * rows, rows), rows), :],
                sem_bias_s.at[item, o], sem_bias_r.at[item, o], res_peer(o), my_h,
            )
        return make

    def bins_block(r):
        return pl.ds(pl.multiple_of((r * rows) // 128 * 128, 128), 128)

    def bins_copy(o):
        return send(
            bins_low.at[:, :, bins_block(res_peer(o))], bins_in.at[my_r],
            sem_bins_s.at[o], sem_bins_r.at[o], res_peer(o), my_h,
        )

    def we_copy(o):
        at = (slice(None), pl.ds(pl.multiple_of(my_h * unit, unit), unit))
        return send(we.at[at], we.at[at], sem_w_s.at[0, o], sem_w_r.at[0, o], my_r, head_peer(o))

    def wr_copy(o):
        at = pl.ds(pl.multiple_of(my_h * unit, unit), unit)
        return send(wr.at[at], wr.at[at], sem_w_s.at[1, o], sem_w_r.at[1, o], my_r, head_peer(o))

    def wo_copy(o):
        at = pl.ds(pl.multiple_of(my_h * width, width), width)
        return send(wo.at[at], wo.at[at], sem_w_s.at[2, o], sem_w_r.at[2, o], my_r, head_peer(o))

    def gated_copy(item):
        def make(o):
            p = head_peer(o)
            return send(
                gated.at[item, pl.ds(p * own, own)],
                gall.at[item, :, pl.ds(pl.multiple_of(my_h * width, width), width), :],
                sem_gat_s.at[item, o], sem_gat_r.at[item, o], my_r, p,
            )
        return make

    def attend(item):
        live = iota((length, length), 0) < lengths[item]
        bt = dot(ident_l, bias_all[item], NT) * LOG2E
        bias_t[...] = bt + jnp.where(live, 0.0, NEG * LOG2E)

        def row(r):
            q = qkv[item, r, 0:width].astype(F32) * (scale * LOG2E)
            hi = q.astype(LOW)
            lo = (q - hi.astype(F32)).astype(LOW)
            rhs = jnp.concatenate([hi, lo, jnp.zeros((2 * width, length), LOW)], 0)
            s = dot(tok[item, r], rhs) + bias_t[...]
            e = jnp.exp2(s - jnp.max(s, 0, keepdims=True)).astype(LOW)
            expo[item, r] = e
            lhs = jnp.concatenate(
                [qkv[item, r, 2 * width : 3 * width], jnp.ones((16, length), LOW)], 0
            )
            o = dot(lhs, e)
            inv = 1.0 / o[width : width + 1]
            rinv[item, pl.ds(r, 1), :] = inv
            m = o[:width] * inv
            mixed[item, r] = m
            gated[item, r] = (m * sig[item, r]).astype(LOW)

        def chunk(o, carry):
            p = head_peer(o)

            def one(k, c):
                row(p * own + k)
                return c
            lax.fori_loop(0, own, one, 0, unroll=4)

            @pl.when(o < heads)
            def _():
                gated_copy(item)(o).start()
            return carry
        lax.fori_loop(1, heads + 1, chunk, 0)
        gall[item, :, pl.ds(pl.multiple_of(my_h * width, width), width), :] = gated[
            item, pl.ds(my_h * own, own)
        ]

    def pair_of(ref, item, t):
        return jnp.concatenate([ref[item, t], ref[item, t + half_own]], 1)

    sel_row = iota((total * half_own, length), 0)
    sel_col = iota((total * half_own, length), 1)
    sel_at = sel_row // half_own * own + lax.rem(sel_row, half_own)
    sel_a = (sel_col == sel_at).astype(F32).astype(LOW)
    sel_b = (sel_col == sel_at + half_own).astype(F32).astype(LOW)

    def forward(item):
        def tile(t, carry):
            g2 = pair_of(gall, item, t)
            base = my_h * own + t
            first = jnp.concatenate(
                [dot(ident, pair[item, base], NT), dot(ident, pair[item, base + half_own], NT)], 1
            ) + dot(wot[...], g2)
            center = first - jnp.mean(first, 0, keepdims=True)
            rs = lax.rsqrt(jnp.mean(center * center, 0, keepdims=True) + EPS)
            xh = center * rs
            xhat[item, t] = xh
            rstd[item, t] = jnp.broadcast_to(rs, (8, 2 * length))
            gc = jnp.concatenate([gain_col[...]] * (2 * length // chan), 1)
            wid = (xh * gc).astype(LOW)
            widened[item, t] = wid
            for b in range(heads):
                hidden[item, t, b * unit : (b + 1) * unit] = jnp.maximum(
                    dot(wet[b * unit : (b + 1) * unit], wid), 0.0
                ).astype(LOW)
            second = (first + dot(wrt[...], hidden[item, t])).astype(LOW)
            slow[item, t] = second
            half = dot(wdt[...], second)
            zero = jnp.zeros((nbins, length), LOW)
            for k in range(2):
                part = half[:, k * length : (k + 1) * length]
                halves[item, t + k * half_own] = part
                part = part.astype(LOW)
                packed = dot(sel_a, jnp.concatenate([part, zero], 0), NT) + dot(
                    sel_b, jnp.concatenate([zero, part], 0), NT
                )
                pack_f[pl.ds(t + k * half_own, total * half_own, own), :] = packed
            return carry
        lax.fori_loop(0, half_own, tile, 0)
        half_send[item] = pack_f[...].reshape(half_send.shape[1:]).astype(LOW)
        half_in[item, me] = half_send[item, me]

    def half_copy(item):
        def make(o):
            d, r, h = any_peer(o)
            return send(
                half_send.at[item, d], half_in.at[item, me],
                sem_half_s.at[item, o], sem_half_r.at[item, o], r, h,
            )
        return make

    size_sum = jnp.zeros((1, length), F32)
    for item in range(items):
        size = lengths[item]
        size_sum = size_sum + (jnp.zeros((1, length), jnp.int32) + size * size).astype(F32)

    def backward(item):
        mirror[...] = half_in[item].astype(F32)
        live = (iota((1, length), 1) < lengths[item]).astype(F32) / size_sum
        levels = iota((nbins, length), 0).astype(F32)[None]

        def tile(t, carry):
            flip = mirror[:, pl.ds(pl.multiple_of(t * own, own), own), :].reshape(length, 2 * nbins)
            flip = dot(eye(2 * nbins), flip.astype(LOW), NT)
            here = jnp.concatenate([halves[item, t], halves[item, t + half_own]], 0)
            logits = (here + flip).reshape(2, nbins, length) + jnp.concatenate(
                [dist_col[...]] * (length // chan), 1
            )[None]
            peak = jnp.max(logits, 1, keepdims=True)
            ex = jnp.exp(logits - peak)
            tot = jnp.sum(ex, 1, keepdims=True)
            prob = ex * (1.0 / tot)

            def two(ref):
                return jnp.concatenate(
                    [ref[item, pl.ds(t, 1), :][None], ref[item, pl.ds(t + half_own, 1), :][None]], 0
                )
            hot = (two(bins_own) == levels).astype(F32)
            hot_t = (two(bins_t) == levels).astype(F32)
            at = me * own + t + iota((2, 1, length), 0) * half_own
            weight = jnp.where(at < lengths[item], 1.0, 0.0) * live[None]
            picked = jnp.sum(hot * logits, 1, keepdims=True)
            lost = weight * (peak + jnp.log(tot) - picked)
            loss_acc[...] += lost[0] + lost[1]
            short = prob - hot
            dl = short * weight
            dist_acc[...] += dl[0] + dl[1]
            dh = ((short + prob - hot_t) * weight).astype(LOW)
            dh2 = jnp.concatenate([dh[0], dh[1]], 1)
            low2 = slow[item, t]
            g_dist[...] += dot(dh2, low2, NT)
            dsec = dot(wd[...], dh2)
            dtr = dsec.astype(LOW)
            wid = widened[item, t]
            for b in range(heads):
                at_b = slice(b * unit, (b + 1) * unit)
                hid = hidden[item, t, at_b]
                dp = jnp.where(hid.astype(F32) > 0.0, dot(wr[at_b], dtr), 0.0).astype(LOW)
                g_red[at_b] += dot(hid, dtr, NT)
                g_exp[at_b] += dot(dp, wid, NT)
                dpre_s[at_b] = dp
            gc = jnp.concatenate([gain_col[...]] * (2 * length // chan), 1)
            dxh = dot(we[...], dpre_s[...]) * gc
            xh = xhat[item, t]
            m1 = jnp.mean(dxh, 0, keepdims=True)
            m2 = jnp.mean(dxh * xh, 0, keepdims=True)
            dout = (dsec + rstd[item, t, 0:1] * (dxh - m1 - xh * m2)).astype(LOW)
            g_out[...] += dot(pair_of(gall, item, t), dout, NT)
            dg = dot(wo[...], dout).astype(LOW)
            for h in range(heads):
                for k in range(2):
                    dg_send[item, h, t + k * half_own] = dg[
                        h * width : (h + 1) * width, k * length : (k + 1) * length
                    ]
            return carry
        lax.fori_loop(0, half_own, tile, 0)
        dg_in[item, pl.ds(my_h * own, own)] = dg_send[item, my_h]

    def dg_copy(item):
        def make(o):
            p = head_peer(o)
            return send(
                dg_send.at[item, p], dg_in.at[item, pl.ds(my_h * own, own)],
                sem_dg_s.at[item, o], sem_dg_r.at[item, o], my_r, p,
            )
        return make

    def attend_back(item):
        db_acc[...] = jnp.zeros_like(db_acc)
        tail_row = iota((16, length), 0)

        def row(r, carry):
            s = sig[item, r]
            m = mixed[item, r]
            dg = dg_in[item, r].astype(F32)
            dm = (dg * s * rinv[item, pl.ds(r, 1), :]).astype(LOW)
            inner = -jnp.sum(dm.astype(F32) * m, 0, keepdims=True)
            hi = inner.astype(LOW).astype(F32)
            lo = inner - hi
            tail = jnp.where(tail_row == 0, hi, jnp.where(tail_row == 1, lo, 0.0)).astype(LOW)
            rhs = jnp.concatenate(
                [jnp.zeros((2 * width, length), LOW), dm, tail, jnp.zeros((width - 16, length), LOW)], 0
            )
            e = expo[item, r]
            ds = e.astype(F32) * dot(tok[item, r], rhs)
            db_acc[...] += ds
            ds = ds.astype(LOW)
            dq = dot(qkv[item, r, width : 2 * width], ds) * scale
            dk = dot(qkv[item, r, 0:width], ds, NT) * scale
            dv = dot(dm, e, NT)
            dproj = jnp.concatenate([dq, dk, dv, dg * m * s * (1.0 - s)], 0).astype(LOW)
            g_head[...] += dot(dproj, normed[item, r])
            return carry
        lax.fori_loop(0, rows, row, 0, unroll=4)
        db_send[item] = dot(ident_l, db_acc[...].astype(LOW), NT).astype(LOW)
        db_in[item, my_r] = db_send[item, pl.ds(pl.multiple_of(my_r * rows, rows), rows), :]

    def db_copy(item):
        def make(o):
            p = res_peer(o)
            return send(
                db_send.at[item, pl.ds(pl.multiple_of(p * rows, rows), rows), :], db_in.at[item, my_r],
                sem_db_s.at[item, o], sem_db_r.at[item, o], p, my_h,
            )
        return make

    def bias_back(item):
        db = db_in[item, 0].astype(F32)
        for s in range(1, groups):
            db = db + db_in[item, s].astype(F32)
        db = db.astype(LOW).astype(F32)
        at = iota((rows, length), 0)

        def row(r, acc):
            return acc + dot(jnp.where(at == r, db, 0.0).astype(LOW), normed[item, r])
        acc = lax.fori_loop(0, rows, row, jnp.zeros((rows, chan), F32), unroll=4)
        g_bias[...] += jnp.sum(acc, 0, keepdims=True)

    def block_copy(o):
        d, r, h = any_peer(o)
        return send(block_send.at[d], block_in.at[me], sem_blk_s.at[o], sem_blk_r.at[o], r, h)

    def gather_copy(o):
        return send(block_sum, o_block.at[my_r], sem_gath_s.at[o], sem_gath_r.at[o], res_peer(o), my_h)

    ru, rw, rb = unit // groups, width // groups, nbins // total

    def block_make():
        for r in range(groups):
            for h in range(heads):
                d = r * heads + h
                at = h * unit + r * ru
                block_send[d, 0:ru] = g_red[at : at + ru]
                block_send[d, ru : 2 * ru] = g_exp[at : at + ru]
                at = h * width + r * rw
                block_send[d, 2 * ru : 2 * ru + rw] = g_out[at : at + rw]
                block_send[d, 2 * ru + rw : 2 * ru + rw + rb] = g_dist[d * rb : (d + 1) * rb]
                block_send[d, 2 * ru + rw + rb :] = jnp.zeros((8 - rw - rb, chan), F32)
        block_in[me] = block_send[me]

    def block_add():
        acc = block_in[0]
        for d in range(1, total):
            acc = acc + block_in[d]
        block_sum[...] = acc
        o_block[my_r] = acc

    def head_copy(o):
        p = res_peer(o)
        return send(
            g_head.at[pl.ds(pl.multiple_of(p * (4 * width // groups), 4 * width // groups), 4 * width // groups), :],
            head_in.at[my_r], sem_head_s.at[o], sem_head_r.at[o], p, my_h,
        )

    def small_copy(o):
        return send(small_own, small_in.at[my_r], sem_small_s.at[o], sem_small_r.at[o], res_peer(o), my_h)

    def card_copy(o):
        d, r, h = any_peer(o)
        return send(card, card_in.at[me], sem_card_s.at[o], sem_card_r.at[o], r, h)

    def fin_copy(o):
        return send(head_sum, o_head.at[my_r], sem_fin_s.at[o], sem_fin_r.at[o], res_peer(o), my_h)

    for ref in (g_out, g_red, g_exp, g_dist, loss_acc, dist_acc, g_head, g_bias):
        ref[...] = jnp.zeros_like(ref)
    before(0)
    pl.semaphore_wait(barrier, total - 1)
    each(groups, bias_copy(0), start)
    for make in (we_copy, wr_copy, wo_copy):
        each(heads, make, start)
    for item in range(1, items):
        before(item)
        each(groups, bias_copy(item), start)
    each(groups, bins_copy, start)
    bins_in[my_r] = bins_low[:, :, bins_block(my_r)]
    for item in range(items):
        each(groups, bias_copy(item), wait_in)
        attend(item)
    for make in (we_copy, wr_copy, wo_copy):
        each(heads, make, wait_in)
    for b in range(heads):
        at = slice(b * unit, (b + 1) * unit)
        wet[at] = dot(ident, we[:, at], NT).astype(LOW)
        wrt[:, at] = dot(ident, wr[at], NT).astype(LOW)
    wot[...] = dot(ident, wo[...], NT).astype(LOW)
    for item in range(items):
        each(heads, gated_copy(item), wait_in)
        forward(item)
        each(total, half_copy(item), start)
    each(groups, bins_copy, wait_in)
    lane = my_r * rows + my_h * own - (my_r * rows) // 128 * 128
    pick = (iota((16, 128), 1) == iota((16, 128), 0) + lane).astype(F32).astype(LOW)
    for item in range(items):
        bins_t[item] = dot(pick, bins_in[:, item].reshape(groups * rows, 128), NT)
    for item in range(items):
        each(total, half_copy(item), wait_in)
        backward(item)
        each(heads, dg_copy(item), start)
    block_make()
    each(total, block_copy, start)
    for item in range(items):
        each(heads, dg_copy(item), wait_in)
        attend_back(item)
        each(groups, db_copy(item), start)
        if item == 0:
            each(total, block_copy, wait_in)
            block_add()
            each(groups, gather_copy, start)
    each(groups, head_copy, start)
    sh = 4 * width // groups
    head_in[my_r] = g_head[pl.ds(pl.multiple_of(my_r * sh, sh), sh), :]
    for item in range(items):
        each(groups, db_copy(item), wait_in)
        bias_back(item)
    gb = g_bias[...]
    up_one = jnp.sum(wc[0 : 4 * width].astype(F32) * g_head[...], 0, keepdims=True) + brow * gb
    up_two = jnp.sum(wet[...].astype(F32) * g_exp[...], 0, keepdims=True)
    dacc = dist_acc[:, 0:chan]
    lacc = loss_acc[:, 0:chan]
    for k in range(1, length // chan):
        dacc = dacc + dist_acc[:, k * chan : (k + 1) * chan]
        lacc = lacc + loss_acc[:, k * chan : (k + 1) * chan]
    dacc = jnp.transpose(jnp.concatenate([dacc, jnp.zeros((chan - nbins, chan), F32)], 0))
    small_own[0:1] = gb
    small_own[1:2] = up_one / gain_one
    small_own[2:3] = up_two / gain_two
    small_own[3:4] = jnp.sum(dacc, 0, keepdims=True)
    small_own[4:5] = lacc
    small_own[5:8] = jnp.zeros((3, chan), F32)
    small_in[my_r] = small_own[...]
    each(groups, small_copy, start)
    each(groups, head_copy, wait_in)
    acc = head_in[0]
    for s in range(1, groups):
        acc = acc + head_in[s]
    head_sum[...] = acc
    o_head[my_r] = acc
    each(groups, fin_copy, start)
    each(groups, small_copy, wait_in)
    tiny = small_in[0]
    for s in range(1, groups):
        tiny = tiny + small_in[s]
    blocks = block_sum[...]
    squares = jnp.sum(acc * acc, 0, keepdims=True) + jnp.sum(blocks * blocks, 0, keepdims=True)
    card[...] = tiny
    card[5:6] = squares
    card[6:8] = blocks[2 * ru + rw : 2 * ru + rw + rb]
    card_in[me] = card[...]
    each(total, card_copy, start)
    each(total, card_copy, wait_in)
    every = card_in[0]
    for d in range(1, total):
        every = every + card_in[d]
    mine = [card_in[my_r * heads + h] for h in range(heads)]
    summed = mine[0]
    bias_sq = mine[0] * mine[0]
    for h in range(1, heads):
        summed = summed + mine[h]
        bias_sq = bias_sq + mine[h] * mine[h]
    norm_sq = every[5:6] + bias_sq[0:1]
    for k in (1, 2, 3):
        norm_sq = norm_sq + summed[k : k + 1] * summed[k : k + 1]
    norm = jnp.sqrt(jnp.sum(norm_sq, -1, keepdims=True))
    o_small[...] = summed
    o_small[0:1] = card[0:1]
    o_small[4:5] = jnp.broadcast_to(jnp.sum(summed[4:5], -1, keepdims=True), (1, chan))
    o_small[5:6] = jnp.broadcast_to(norm, (1, chan))
    o_small[6:7] = jnp.broadcast_to(CLIP / jnp.maximum(norm, CLIP), (1, chan))
    for d in range(total):
        o_dist[d * rb : (d + 1) * rb] = card_in[d, 6 : 6 + rb]
    each(groups, gather_copy, wait_in)
    each(groups, fin_copy, wait_in)
    for item in range(items):
        each(groups, bias_copy(item), wait_out)
        each(heads, gated_copy(item), wait_out)
        each(total, half_copy(item), wait_out)
        each(heads, dg_copy(item), wait_out)
        each(groups, db_copy(item), wait_out)
    for make in (we_copy, wr_copy, wo_copy):
        each(heads, make, wait_out)
    for make in (bins_copy, gather_copy, head_copy, small_copy, fin_copy):
        each(groups, make, wait_out)
    for make in (block_copy, card_copy):
        each(total, make, wait_out)


def update_kernel(groups, *refs):
    g_head, g_block, g_dist, g_small = refs[:4]
    weights, momenta, averages = refs[4:11], refs[11:18], refs[18:25]
    loss, norm = refs[25:27]
    new_w, new_m, new_a = refs[27:34], refs[34:41], refs[41:48]
    loss[...] = g_small[4:5, 0:1]
    norm[...] = g_small[5:6, 0:1]
    factor = g_small[6:7, 0:1]
    unit = weights[4].shape[0]
    width = weights[2].shape[0]
    ru, rw = unit // groups, width // groups
    chan = g_small.shape[1]

    def put(k, grad, at=(slice(None), slice(None))):
        fresh, velocity, average = advance(
            weights[k][at], momenta[k][at], averages[k][at], grad * factor
        )
        new_w[k][at] = fresh
        new_m[k][at] = velocity
        new_a[k][at] = average

    put(0, jnp.transpose(g_head[...].reshape(weights[0].shape[1], chan)))
    put(1, g_small[0:1])
    put(3, jnp.transpose(g_block[:, ru : 2 * ru].reshape(unit, chan)))
    put(4, g_block[:, 0:ru].reshape(unit, chan))
    for r in range(groups):
        put(2, g_block[r, 2 * ru : 2 * ru + rw], (slice(r * rw, (r + 1) * rw), slice(None)))
    nbins = weights[5].shape[1]
    put(5, jnp.transpose(jnp.concatenate([g_dist[...], jnp.zeros((chan - nbins, chan), F32)], 0))[:, :nbins])
    put(6, g_small[1:2], (slice(None), slice(0, chan)))
    put(6, g_small[2:3], (slice(None), slice(chan, 2 * chan)))
    put(6, g_small[3:4, 0:nbins], (slice(None), slice(2 * chan, 2 * chan + nbins)))


def fused_body(groups, heads, *args):
    pair_input, lengths, distogram_bins = args[:3]
    weights, momenta, averages = list(args[3:10]), list(args[10:17]), list(args[17:24])
    items, rows, length, chan = pair_input.shape
    width = weights[2].shape[0]
    unit = weights[3].shape[1]
    nbins = weights[5].shape[1]
    own, total = rows // heads, groups * heads
    half_own = own // 2
    for group in (weights, momenta, averages):
        group[1] = group[1].reshape(1, chan)
        group[6] = group[6].reshape(1, -1)
    small = jnp.pad(weights[6], ((0, 0), (0, 3 * chan - weights[6].shape[1])))
    vmem = pl.BlockSpec(memory_space=pltpu.VMEM)
    block_rows = 2 * (unit // groups) + 8
    sh = 4 * width // groups
    V = pltpu.VMEM
    dma = pltpu.SemaphoreType.DMA
    scratch = [
        V((items, rows, length, chan), LOW),
        V((items, rows, length, 4 * width), LOW),
        V((items, rows, 3 * width, length), LOW),
        V((items, rows, width, length), F32),
        V((items, rows, length, length), LOW),
        V((items, rows, width, length), F32),
        V((items, rows, length), F32),
        V((4 * width + 16, chan), LOW),
        V((chan, 4 * width), LOW),
        V((chan, heads * unit), LOW),
        V((heads * unit, chan), LOW),
        V((heads * unit, chan), LOW),
        V((chan, heads * unit), LOW),
        V((heads * width, chan), LOW),
        V((chan, heads * width), LOW),
        V((chan, nbins), LOW),
        V((nbins, chan), LOW),
        V((chan, chan), F32),
        V((nbins, chan), F32),
        V((rows, length), F32),
        V((items, rows, length), LOW),
        V((items, length, length), LOW),
        V((length, length), F32),
        V((items, rows, length), LOW),
        V((groups, items, rows, 128), LOW),
        V((items, own, length), F32),
        V((items, 16, length), F32),
        V((items, rows, width, length), LOW),
        V((items, own, heads * width, length), LOW),
        V((items, half_own, chan, 2 * length), F32),
        V((items, half_own, 8, 2 * length), F32),
        V((items, half_own, chan, 2 * length), LOW),
        V((items, half_own, heads * unit, 2 * length), LOW),
        V((items, half_own, chan, 2 * length), LOW),
        V((items, own, nbins, length), F32),
        V((total * half_own * own, 2 * nbins), F32),
        V((items, total, half_own * own, 2 * nbins), LOW),
        V((items, total, half_own * own, 2 * nbins), LOW),
        V((total, half_own * own, 2 * nbins), F32),
        V((heads * unit, 2 * length), LOW),
        V((items, heads, own, width, length), LOW),
        V((items, rows, width, length), LOW),
        V((heads * width, chan), F32),
        V((heads * unit, chan), F32),
        V((heads * unit, chan), F32),
        V((nbins, chan), F32),
        V((1, length), F32),
        V((nbins, length), F32),
        V((total, block_rows, chan), F32),
        V((total, block_rows, chan), F32),
        V((block_rows, chan), F32),
        V((length, length), F32),
        V((items, length, length), LOW),
        V((items, groups, rows, length), LOW),
        V((4 * width, chan), F32),
        V((1, chan), F32),
        V((groups, sh, chan), F32),
        V((sh, chan), F32),
        V((8, chan), F32),
        V((groups, 8, chan), F32),
        V((8, chan), F32),
        V((total, 8, chan), F32),
    ]
    for shape in (
        (items, groups), (groups,), (3, heads), (items, heads), (items, total), (items, heads),
        (total,), (groups,), (items, groups), (groups,), (groups,), (total,), (groups,),
    ):
        scratch += [dma(shape), dma(shape)]
    grads = pl.pallas_call(
        partial(step_kernel, groups, heads),
        out_shape=[
            jax.ShapeDtypeStruct((groups, sh, chan), F32),
            jax.ShapeDtypeStruct((groups, block_rows, chan), F32),
            jax.ShapeDtypeStruct((nbins, chan), F32),
            jax.ShapeDtypeStruct((8, chan), F32),
        ],
        in_specs=[vmem, pl.BlockSpec(memory_space=pltpu.SMEM)] + [vmem] * 8,
        out_specs=[vmem] * 4,
        scratch_shapes=scratch,
        compiler_params=pltpu.CompilerParams(
            collective_id=0, has_side_effects=True, vmem_limit_bytes=60 * 2**20
        ),
        name="step",
    )(pair_input, lengths, distogram_bins, *weights[:6], small)
    like = lambda group: [jax.ShapeDtypeStruct(w.shape, F32) for w in group]
    outs = pl.pallas_call(
        partial(update_kernel, groups),
        out_shape=[jax.ShapeDtypeStruct((1, 1), F32)] * 2 + like(weights) * 3,
        in_specs=[vmem] * 25,
        out_specs=[vmem] * 23,
        name="update",
    )(*grads, *weights, *momenta, *averages)
    outs = list(outs)
    outs[0], outs[1] = outs[0].reshape(()), outs[1].reshape(())
    for k in (2, 9, 16):
        outs[k + 1] = outs[k + 1].reshape(chan, 1)
        outs[k + 6] = outs[k + 6].reshape(-1)
    return tuple(outs)


def body(groups, heads, *args):
    items, rows, length, channels = args[0].shape
    own = rows // heads
    if own == 8 and rows % 16 == 0 and length % 128 == 0:
        return fused_body(groups, heads, *args)
    return general_body(*args)


def solution(mesh):
    in_specs = (
        P(None, "res", None, None),
        P(),
        P(None, "res", None),
        P(None, "head"),
        P(None, "head"),
        P("head", None),
        P(None, "head"),
        P("head", None),
        P(),
        P(),
        P(None, "head"),
        P(None, "head"),
        P("head", None),
        P(None, "head"),
        P("head", None),
        P(),
        P(),
        P(None, "head"),
        P(None, "head"),
        P("head", None),
        P(None, "head"),
        P("head", None),
        P(),
        P(),
    )
    out_specs = (
        P(),
        P(),
        P(None, "head"),
        P(None, "head"),
        P("head", None),
        P(None, "head"),
        P("head", None),
        P(),
        P(),
        P(None, "head"),
        P(None, "head"),
        P("head", None),
        P(None, "head"),
        P("head", None),
        P(),
        P(),
        P(None, "head"),
        P(None, "head"),
        P("head", None),
        P(None, "head"),
        P("head", None),
        P(),
        P(),
    )
    return jax.shard_map(
        partial(body, mesh.shape["res"], mesh.shape["head"]), mesh=mesh, in_specs=in_specs, out_specs=out_specs, check_vma=False)
```

profile of v0, /device:TPU:0, one launch (start us, length us, event | category | flops | bytes accessed | tf_op | source)
XLA Modules:
  0.0 138.6 jit_solution(13494226531600555817)
XLA Ops:
  0.7 0.7 reshape.89.refs_10_
  1.3 0.0 copy-start
  1.3 0.6 pad.4.refs_9_
  1.9 1.2 reshape.91.refs_17_
  3.2 1.2 reshape.93.refs_24_
  4.4 1.5 %copy.47.refs_8_.refs_9_ = f32[128,64]{1,0:T(8,128)} copy(f32[128,64]{0,1:T(8,128)} %param.32) | data formatting | bytes 65536 | tf_op args[8]
  5.9 1.5 %copy.49.refs_16_ = f32[128,64]{1,0:T(8,128)} copy(f32[128,64]{0,1:T(8,128)} %param.39) | data formatting | bytes 65536 | tf_op args[15]
  7.4 1.5 %copy.50.refs_23_ = f32[128,64]{1,0:T(8,128)} copy(f32[128,64]{0,1:T(8,128)} %param.46) | data formatting | bytes 65536 | tf_op args[22]
  8.8 118.8 %step.1 = (f32[8,16,128]{2,1,0:T(8,128)}, f32[8,40,128]{2,1,0:T(8,128)}, f32[64,128]{1,0:T(8,128)}, f32[8,128]{1,0:T(8,128)}) custom-call(bf16[2,32,256,128]{3,2,1,0:T(8,128)(2,1)} %refs_0_.1, s32[2]{0:T(128)} %refs_1_.1, s32[2,32,256]{2,1,0:T(8,128)} %refs_2_.1, f32[128,128]{1,0:T(8,128)} %refs_4_.1, f32[1,128]{1,0:T(1,128)} %bitcast.8, f32[32,128]{1,0:T(8,128)} %refs_6_.3, ...), custom_call_target="tpu_custom_call" | custom-call | tf_op jit(solution)/shard_map/step/pallas_call | solution.py:960
  127.7 0.0 copy-done
  127.7 2.4 %update.1 = (f32[1,1]{1,0:T(1,128)}, f32[1,1]{1,0:T(1,128)}, f32[128,128]{1,0:T(8,128)}, f32[1,128]{1,0:T(1,128)}, f32[32,128]{1,0:T(8,128)}, /*index=5*/f32[128...) custom-call(f32[8,16,128]{2,1,0:T(8,128)} %get-tuple-element.50.refs, ...), custom_call_target="tpu_custom_call" | custom-call | tf_op jit(solution)/shard_map/update/pallas_call | solution.py:977
  130.1 1.3 reduce
  131.4 1.3 reduce.1
  132.7 1.3 reduce.2
  133.9 1.5 %copy.51 = f32[128,64]{0,1:T(8,128)} copy(f32[128,64]{1,0:T(8,128)} %get-tuple-element.84) | data formatting | bytes 65536
  135.5 1.5 %copy.52 = f32[128,64]{0,1:T(8,128)} copy(f32[128,64]{1,0:T(8,128)} %get-tuple-element.91) | data formatting | bytes 65536
  137.0 1.5 %copy.53 = f32[128,64]{0,1:T(8,128)} copy(f32[128,64]{1,0:T(8,128)} %get-tuple-element.98) | data formatting | bytes 65536
Async XLA Ops:
  1.3 126.3 %copy-start = (f32[1,320]{1,0:T(1,128)}, f32[1,320]{1,0:T(1,128)S(1)}, u32[]{:S(2)}) copy-start(f32[1,320]{1,0:T(1,128)S(1)} %reshape.89.refs_10_) | copy-start | bytes 3844
where the time goes:
time: 139 us
  Pallas kernels  121 us (87%)
  local copies, waits for them, and re-layouts  12.8 us (9%)
  other arithmetic  3.82 us (3%)
    pallas_call x1, Pallas kernels, fused_body(): pl.pallas_call(partial(step_kernel, groups, heads), out_shape=[jax.ShapeD...  119 us
    unnamed x8, local copies, waits for them, and re-layouts  9.05 us
    pallas_call x3, other arithmetic, fused_body(): pl.pallas_call(partial(update_kernel, groups), out_shape=[jax.ShapeDtypeS...  3.82 us
    reshape x3, local copies, waits for them, and re-layouts, fused_body(): group[6] = group[6].reshape(1, -1)  3.17 us

commit v1 on v0

--- a/solution.py
+++ b/solution.py
@@ -297,6 +297,13 @@
     return 0.5 * jnp.tanh(0.5 * x) + 0.5
 
 
+def staged(count, stages, lag):
+    for step in range(count + lag * (len(stages) - 1)):
+        for k, stage in enumerate(stages):
+            if 0 <= step - k * lag < count:
+                stage(step - k * lag)
+
+
 def step_kernel(groups, heads, *refs):
     (
         pair, lengths, bins, head_w, bias_w, out_w, exp_w, red_w, dist_w, small,
@@ -305,9 +312,9 @@
         wc, wt, we, wet, wr, wrt, wo, wot, wd, wdt, gain_col, dist_col,
         bias_f, bias_send, bias_all, bias_t, bins_low, bins_in, bins_own, bins_t,
         gated, gall, xhat, rstd, widened, hidden, slow, halves, pack_f, half_send, half_in, mirror,
-        dpre_s, dg_send, dg_in, g_out, g_red, g_exp, g_dist, loss_acc, dist_acc,
+        dpre_s, first_s, dh_s, dsec_s, dtr_s, dout_s, dg_send, dg_in, g_out, g_red, g_exp, g_dist, loss_acc, dist_acc,
         block_send, block_in, block_sum,
-        db_acc, db_send, db_in, g_head, g_bias, head_in, head_sum, small_own, small_in, card, card_in,
+        db_acc, ds_s, dm_s, dproj_s, db_send, db_in, g_head, g_bias, head_in, head_sum, small_own, small_in, card, card_in,
         sem_bias_s, sem_bias_r, sem_bins_s, sem_bins_r, sem_w_s, sem_w_r,
         sem_gat_s, sem_gat_r, sem_half_s, sem_half_r, sem_dg_s, sem_dg_r,
         sem_blk_s, sem_blk_r, sem_gath_s, sem_gath_r, sem_db_s, sem_db_r,
@@ -315,7 +322,7 @@
     ) = refs
     items, rows, length, chan = pair.shape
     width = out_w.shape[0]
-    nbins = dist_w.shape[1]
+    nbins = dist_w.shape[0]
     unit = exp_w.shape[1]
     own = rows // heads
     half_own = own // 2
@@ -376,33 +383,45 @@
     wt[...] = dot(hw_low, (src_col == want).astype(F32).astype(LOW)).astype(LOW)
     ident = eye(chan)
     ident_l = eye(length)
-    gain_one = small[:, 0:chan]
-    gain_two = small[:, chan : 2 * chan]
+    center_by = (ident.astype(F32) - 1.0 / chan).astype(LOW)
+    gain_one = small[0:chan].reshape(1, chan)
+    gain_two = small[chan : 2 * chan].reshape(1, chan)
+    bins_row = jnp.concatenate(
+        [small[2 * chan : 2 * chan + nbins].reshape(1, nbins), jnp.zeros((1, chan - nbins), F32)], 1
+    )
     gain_col[...] = jnp.transpose(jnp.broadcast_to(gain_two, (chan, chan)))
-    dist_col[...] = jnp.transpose(jnp.broadcast_to(small[:, 2 * chan : 3 * chan], (chan, chan)))[:nbins]
+    dist_col[...] = jnp.transpose(jnp.broadcast_to(bins_row, (chan, chan)))[:nbins]
     we[:, pl.ds(pl.multiple_of(my_h * unit, unit), unit)] = exp_w[...].astype(LOW)
     wr[pl.ds(pl.multiple_of(my_h * unit, unit), unit), :] = red_w[...].astype(LOW)
     wo[pl.ds(pl.multiple_of(my_h * width, width), width), :] = out_w[...].astype(LOW)
-    wd[...] = dist_w[...].astype(LOW)
-    wdt[...] = dot(eye(nbins), wd[...], NT).astype(LOW)
+    wdt[...] = dist_w[...].astype(LOW)
+    wd[...] = dot(ident, wdt[...], NT).astype(LOW)
     bins_low[...] = bins[...].astype(F32).astype(LOW)
     bins_own[...] = bins[:, pl.ds(pl.multiple_of(my_h * own, own), own), :].astype(F32)
     one_lane = (iota((1, 4 * width), 1) >= 3 * width).astype(F32)
 
     def before(item):
-        def row(r, carry):
-            x = pair[item, r].astype(F32)
-            center = x - jnp.mean(x, -1, keepdims=True)
+        def norm(r):
+            center = dot(pair[item, r], center_by)
             spread = jnp.mean(center * center, -1, keepdims=True)
-            low = (center * lax.rsqrt(spread + EPS) * gain_one).astype(LOW)
-            normed[item, r] = low
+            normed[item, r] = (center * lax.rsqrt(spread + EPS) * gain_one).astype(LOW)
+
+        def mult(r):
+            low = normed[item, r]
             ch = dot(wc[...], low, NT)
             qkv[item, r] = ch[: 3 * width].astype(LOW)
             sig[item, r] = sigmoid(ch[3 * width : 4 * width])
             bias_f[pl.ds(r, 1), :] = ch[4 * width : 4 * width + 1]
             tok[item, r] = (dot(low, wt[...]) + one_lane).astype(LOW)
+
+        def group(t, carry):
+            for k in range(8 + 8):
+                if k < 8:
+                    norm(t * 8 + k)
+                if k >= 8:
+                    mult(t * 8 + k - 8)
             return carry
-        lax.fori_loop(0, rows, row, 0, unroll=2)
+        lax.fori_loop(0, rows // 8, group, 0)
         bias_send[item] = bias_f[...].astype(LOW)
         bias_all[item, pl.ds(pl.multiple_of(my_r * rows, rows), rows), :] = bias_f[...].astype(LOW)
 
@@ -451,18 +470,19 @@
         bt = dot(ident_l, bias_all[item], NT) * LOG2E
         bias_t[...] = bt + jnp.where(live, 0.0, NEG * LOG2E)
 
-        def row(r):
+        def scores(r):
             q = qkv[item, r, 0:width].astype(F32) * (scale * LOG2E)
             hi = q.astype(LOW)
             lo = (q - hi.astype(F32)).astype(LOW)
             rhs = jnp.concatenate([hi, lo, jnp.zeros((2 * width, length), LOW)], 0)
             s = dot(tok[item, r], rhs) + bias_t[...]
-            e = jnp.exp2(s - jnp.max(s, 0, keepdims=True)).astype(LOW)
-            expo[item, r] = e
+            expo[item, r] = jnp.exp2(s - jnp.max(s, 0, keepdims=True)).astype(LOW)
+
+        def gather(r):
             lhs = jnp.concatenate(
                 [qkv[item, r, 2 * width : 3 * width], jnp.ones((16, length), LOW)], 0
             )
-            o = dot(lhs, e)
+            o = dot(lhs, expo[item, r])
             inv = 1.0 / o[width : width + 1]
             rinv[item, pl.ds(r, 1), :] = inv
             m = o[:width] * inv
@@ -471,11 +491,16 @@
 
         def chunk(o, carry):
             p = head_peer(o)
-
-            def one(k, c):
-                row(p * own + k)
+            base = p * own
+
+            def one(t, c):
+                for k in range(8 + 4):
+                    if k < 8:
+                        scores(base + t * 8 + k)
+                    if k >= 4:
+                        gather(base + t * 8 + k - 4)
                 return c
-            lax.fori_loop(0, own, one, 0, unroll=4)
+            lax.fori_loop(0, own // 8, one, 0, unroll=1)
 
             @pl.when(o < heads)
             def _():
@@ -496,38 +521,46 @@
     sel_b = (sel_col == sel_at + half_own).astype(F32).astype(LOW)
 
     def forward(item):
-        def tile(t, carry):
+        gc = jnp.concatenate([gain_col[...]] * (2 * length // chan), 1)
+        zero = jnp.zeros((nbins, length), LOW)
+
+        def enter(t):
             g2 = pair_of(gall, item, t)
             base = my_h * own + t
             first = jnp.concatenate(
                 [dot(ident, pair[item, base], NT), dot(ident, pair[item, base + half_own], NT)], 1
             ) + dot(wot[...], g2)
+            first_s[t] = first
             center = first - jnp.mean(first, 0, keepdims=True)
             rs = lax.rsqrt(jnp.mean(center * center, 0, keepdims=True) + EPS)
             xh = center * rs
             xhat[item, t] = xh
             rstd[item, t] = jnp.broadcast_to(rs, (8, 2 * length))
-            gc = jnp.concatenate([gain_col[...]] * (2 * length // chan), 1)
-            wid = (xh * gc).astype(LOW)
-            widened[item, t] = wid
+            widened[item, t] = (xh * gc).astype(LOW)
+
+        def expand(t):
             for b in range(heads):
                 hidden[item, t, b * unit : (b + 1) * unit] = jnp.maximum(
-                    dot(wet[b * unit : (b + 1) * unit], wid), 0.0
+                    dot(wet[b * unit : (b + 1) * unit], widened[item, t]), 0.0
                 ).astype(LOW)
-            second = (first + dot(wrt[...], hidden[item, t])).astype(LOW)
-            slow[item, t] = second
-            half = dot(wdt[...], second)
-            zero = jnp.zeros((nbins, length), LOW)
+
+        def reduce(t):
+            slow[item, t] = (first_s[t] + dot(wrt[...], hidden[item, t])).astype(LOW)
+
+        def project_half(t):
+            half = dot(wdt[...], slow[item, t])
+            halves[item, t] = half[:, :length]
+            halves[item, t + half_own] = half[:, length:]
+
+        def pack(t):
             for k in range(2):
-                part = half[:, k * length : (k + 1) * length]
-                halves[item, t + k * half_own] = part
-                part = part.astype(LOW)
+                part = halves[item, t + k * half_own].astype(LOW)
                 packed = dot(sel_a, jnp.concatenate([part, zero], 0), NT) + dot(
                     sel_b, jnp.concatenate([zero, part], 0), NT
                 )
                 pack_f[pl.ds(t + k * half_own, total * half_own, own), :] = packed
-            return carry
-        lax.fori_loop(0, half_own, tile, 0)
+
+        staged(half_own, (enter, expand, reduce, project_half, pack), 2)
         half_send[item] = pack_f[...].reshape(half_send.shape[1:]).astype(LOW)
         half_in[item, me] = half_send[item, me]
 
@@ -550,24 +583,25 @@
         live = (iota((1, length), 1) < lengths[item]).astype(F32) / size_sum
         levels = iota((nbins, length), 0).astype(F32)[None]
 
-        def tile(t, carry):
-            flip = mirror[:, pl.ds(pl.multiple_of(t * own, own), own), :].reshape(length, 2 * nbins)
+        gc = jnp.concatenate([gain_col[...]] * (2 * length // chan), 1)
+        dist_c = jnp.concatenate([dist_col[...]] * (length // chan), 1)[None]
+
+        def two(ref, t):
+            return jnp.concatenate(
+                [ref[item, pl.ds(t, 1), :][None], ref[item, pl.ds(t + half_own, 1), :][None]], 0
+            )
+
+        def loss_grad(t):
+            flip = mirror[:, t * own : (t + 1) * own, :].reshape(length, 2 * nbins)
             flip = dot(eye(2 * nbins), flip.astype(LOW), NT)
             here = jnp.concatenate([halves[item, t], halves[item, t + half_own]], 0)
-            logits = (here + flip).reshape(2, nbins, length) + jnp.concatenate(
-                [dist_col[...]] * (length // chan), 1
-            )[None]
+            logits = (here + flip).reshape(2, nbins, length) + dist_c
             peak = jnp.max(logits, 1, keepdims=True)
             ex = jnp.exp(logits - peak)
             tot = jnp.sum(ex, 1, keepdims=True)
             prob = ex * (1.0 / tot)
-
-            def two(ref):
-                return jnp.concatenate(
-                    [ref[item, pl.ds(t, 1), :][None], ref[item, pl.ds(t + half_own, 1), :][None]], 0
-                )
-            hot = (two(bins_own) == levels).astype(F32)
-            hot_t = (two(bins_t) == levels).astype(F32)
+            hot = (two(bins_own, t) == levels).astype(F32)
+            hot_t = (two(bins_t, t) == levels).astype(F32)
             at = me * own + t + iota((2, 1, length), 0) * half_own
             weight = jnp.where(at < lengths[item], 1.0, 0.0) * live[None]
             picked = jnp.sum(hot * logits, 1, keepdims=True)
@@ -577,34 +611,45 @@
             dl = short * weight
             dist_acc[...] += dl[0] + dl[1]
             dh = ((short + prob - hot_t) * weight).astype(LOW)
-            dh2 = jnp.concatenate([dh[0], dh[1]], 1)
-            low2 = slow[item, t]
-            g_dist[...] += dot(dh2, low2, NT)
-            dsec = dot(wd[...], dh2)
-            dtr = dsec.astype(LOW)
-            wid = widened[item, t]
+            dh_s[t] = jnp.concatenate([dh[0], dh[1]], 1)
+
+        def enter(t):
+            dsec = dot(wd[...], dh_s[t])
+            dsec_s[t] = dsec
+            dtr_s[t] = dsec.astype(LOW)
+            g_dist[...] += dot(dh_s[t], slow[item, t], NT)
+
+        def through(t):
             for b in range(heads):
                 at_b = slice(b * unit, (b + 1) * unit)
                 hid = hidden[item, t, at_b]
-                dp = jnp.where(hid.astype(F32) > 0.0, dot(wr[at_b], dtr), 0.0).astype(LOW)
-                g_red[at_b] += dot(hid, dtr, NT)
-                g_exp[at_b] += dot(dp, wid, NT)
-                dpre_s[at_b] = dp
-            gc = jnp.concatenate([gain_col[...]] * (2 * length // chan), 1)
-            dxh = dot(we[...], dpre_s[...]) * gc
+                dpre_s[t, at_b] = jnp.where(
+                    hid.astype(F32) > 0.0, dot(wr[at_b], dtr_s[t]), 0.0
+                ).astype(LOW)
+
+        def weights_back(t):
+            for b in range(heads):
+                at_b = slice(b * unit, (b + 1) * unit)
+                g_red[at_b] += dot(hidden[item, t, at_b], dtr_s[t], NT)
+                g_exp[at_b] += dot(dpre_s[t, at_b], widened[item, t], NT)
+
+        def leave(t):
+            dxh = dot(we[...], dpre_s[t]) * gc
             xh = xhat[item, t]
             m1 = jnp.mean(dxh, 0, keepdims=True)
             m2 = jnp.mean(dxh * xh, 0, keepdims=True)
-            dout = (dsec + rstd[item, t, 0:1] * (dxh - m1 - xh * m2)).astype(LOW)
-            g_out[...] += dot(pair_of(gall, item, t), dout, NT)
-            dg = dot(wo[...], dout).astype(LOW)
+            dout_s[t] = (dsec_s[t] + rstd[item, t, 0:1] * (dxh - m1 - xh * m2)).astype(LOW)
+
+        def output_back(t):
+            dg = dot(wo[...], dout_s[t]).astype(LOW)
             for h in range(heads):
                 for k in range(2):
                     dg_send[item, h, t + k * half_own] = dg[
                         h * width : (h + 1) * width, k * length : (k + 1) * length
                     ]
-            return carry
-        lax.fori_loop(0, half_own, tile, 0)
+            g_out[...] += dot(pair_of(gall, item, t), dout_s[t], NT)
+
+        staged(half_own, (loss_grad, enter, through, weights_back, leave, output_back), 2)
         dg_in[item, pl.ds(my_h * own, own)] = dg_send[item, my_h]
 
     def dg_copy(item):
@@ -620,7 +665,7 @@
         db_acc[...] = jnp.zeros_like(db_acc)
         tail_row = iota((16, length), 0)
 
-        def row(r, carry):
+        def first(r, k, tot):
             s = sig[item, r]
             m = mixed[item, r]
             dg = dg_in[item, r].astype(F32)
@@ -632,17 +677,30 @@
             rhs = jnp.concatenate(
                 [jnp.zeros((2 * width, length), LOW), dm, tail, jnp.zeros((width - 16, length), LOW)], 0
             )
-            e = expo[item, r]
-            ds = e.astype(F32) * dot(tok[item, r], rhs)
+            dm_s[k] = dm
+            dproj_s[3 * width :, k * length : (k + 1) * length] = (dg * m * s * (1.0 - s)).astype(LOW)
+            ds = expo[item, r].astype(F32) * dot(tok[item, r], rhs)
             db_acc[...] += ds
-            ds = ds.astype(LOW)
-            dq = dot(qkv[item, r, width : 2 * width], ds) * scale
-            dk = dot(qkv[item, r, 0:width], ds, NT) * scale
-            dv = dot(dm, e, NT)
-            dproj = jnp.concatenate([dq, dk, dv, dg * m * s * (1.0 - s)], 0).astype(LOW)
-            g_head[...] += dot(dproj, normed[item, r])
+            ds_s[k] = ds.astype(LOW)
+            return None
+
+        def second(r, k):
+            at = slice(k * length, (k + 1) * length)
+            ds = ds_s[k]
+            dproj_s[0:width, at] = (dot(qkv[item, r, width : 2 * width], ds) * scale).astype(LOW)
+            dproj_s[width : 2 * width, at] = (dot(qkv[item, r, 0:width], ds, NT) * scale).astype(LOW)
+            dproj_s[2 * width : 3 * width, at] = dot(dm_s[k], expo[item, r], NT).astype(LOW)
+
+        def group(t, carry):
+            tot = None
+            for k in range(8 + 4):
+                if k < 8:
+                    tot = first(t * 8 + k, k, tot)
+                if k >= 4:
+                    second(t * 8 + k - 4, k - 4)
+            g_head[...] += dot(dproj_s[...], normed[item, pl.ds(t * 8, 8)].reshape(8 * length, chan))
             return carry
-        lax.fori_loop(0, rows, row, 0, unroll=4)
+        lax.fori_loop(0, rows // 8, group, 0)
         db_send[item] = dot(ident_l, db_acc[...].astype(LOW), NT).astype(LOW)
         db_in[item, my_r] = db_send[item, pl.ds(pl.multiple_of(my_r * rows, rows), rows), :]
 
@@ -851,7 +909,7 @@
 
     def put(k, grad, at=(slice(None), slice(None))):
         fresh, velocity, average = advance(
-            weights[k][at], momenta[k][at], averages[k][at], grad * factor
+            weights[k][at], momenta[k][at], averages[k][at], grad * (factor if grad.ndim > 1 else factor[0])
         )
         new_w[k][at] = fresh
         new_m[k][at] = velocity
@@ -863,11 +921,11 @@
     put(4, g_block[:, 0:ru].reshape(unit, chan))
     for r in range(groups):
         put(2, g_block[r, 2 * ru : 2 * ru + rw], (slice(r * rw, (r + 1) * rw), slice(None)))
-    nbins = weights[5].shape[1]
-    put(5, jnp.transpose(jnp.concatenate([g_dist[...], jnp.zeros((chan - nbins, chan), F32)], 0))[:, :nbins])
-    put(6, g_small[1:2], (slice(None), slice(0, chan)))
-    put(6, g_small[2:3], (slice(None), slice(chan, 2 * chan)))
-    put(6, g_small[3:4, 0:nbins], (slice(None), slice(2 * chan, 2 * chan + nbins)))
+    nbins = weights[5].shape[0]
+    put(5, g_dist[...])
+    put(6, g_small[1], (slice(0, chan),))
+    put(6, g_small[2], (slice(chan, 2 * chan),))
+    put(6, g_small[3, 0:nbins], (slice(2 * chan, 2 * chan + nbins),))
 
 
 def fused_body(groups, heads, *args):
@@ -881,8 +939,7 @@
     half_own = own // 2
     for group in (weights, momenta, averages):
         group[1] = group[1].reshape(1, chan)
-        group[6] = group[6].reshape(1, -1)
-    small = jnp.pad(weights[6], ((0, 0), (0, 3 * chan - weights[6].shape[1])))
+        group[5] = group[5].T
     vmem = pl.BlockSpec(memory_space=pltpu.VMEM)
     block_rows = 2 * (unit // groups) + 8
     sh = 4 * width // groups
@@ -928,7 +985,12 @@
         V((items, total, half_own * own, 2 * nbins), LOW),
         V((items, total, half_own * own, 2 * nbins), LOW),
         V((total, half_own * own, 2 * nbins), F32),
-        V((heads * unit, 2 * length), LOW),
+        V((half_own, heads * unit, 2 * length), LOW),
+        V((half_own, chan, 2 * length), F32),
+        V((half_own, nbins, 2 * length), LOW),
+        V((half_own, chan, 2 * length), F32),
+        V((half_own, chan, 2 * length), LOW),
+        V((half_own, chan, 2 * length), LOW),
         V((items, heads, own, width, length), LOW),
         V((items, rows, width, length), LOW),
         V((heads * width, chan), F32),
@@ -941,6 +1003,9 @@
         V((total, block_rows, chan), F32),
         V((block_rows, chan), F32),
         V((length, length), F32),
+        V((8, length, length), LOW),
+        V((8, width, length), LOW),
+        V((4 * width, 8 * length), LOW),
         V((items, length, length), LOW),
         V((items, groups, rows, length), LOW),
         V((4 * width, chan), F32),
@@ -972,7 +1037,7 @@
             collective_id=0, has_side_effects=True, vmem_limit_bytes=60 * 2**20
         ),
         name="step",
-    )(pair_input, lengths, distogram_bins, *weights[:6], small)
+    )(pair_input, lengths, distogram_bins, *weights)
     like = lambda group: [jax.ShapeDtypeStruct(w.shape, F32) for w in group]
     outs = pl.pallas_call(
         partial(update_kernel, groups),
@@ -985,7 +1050,7 @@
     outs[0], outs[1] = outs[0].reshape(()), outs[1].reshape(())
     for k in (2, 9, 16):
         outs[k + 1] = outs[k + 1].reshape(chan, 1)
-        outs[k + 6] = outs[k + 6].reshape(-1)
+        outs[k + 5] = outs[k + 5].T
     return tuple(outs)
 
 

time: 139 us -> 92.3 us (0.66)
  Pallas kernels: 121 us -> 91.3 us
  local copies, waits for them, and re-layouts: 12.8 us -> 0 us
  other arithmetic: 3.82 us -> 0 us
    pallas_call x1, Pallas kernels: 119 us -> 89 us  [fused_body(): pl.pallas_call(partial(step_kernel, groups, heads), out_shape=[jax.ShapeD...]
    unnamed x8 -> x0, local copies, waits for them, and re-layouts: 9.05 us -> none
    pallas_call x3 -> x0, other arithmetic: 3.82 us -> none  [fused_body(): pl.pallas_call(partial(update_kernel, groups), out_shape=[jax.ShapeDtypeS...]
    reshape x3 -> x0, local copies, waits for them, and re-layouts: 3.17 us -> none  [fused_body(): group[6] = group[6].reshape(1, -1)]
where the time goes in v1:
time: 92.3 us; the launch traced here: 92.2 us
  Pallas kernels  91.3 us (99%)
    pallas_call x1, Pallas kernels, fused_body(): pl.pallas_call(partial(step_kernel, groups, heads), out_shape=[jax.ShapeD...  89 us
    pallas_call x1, Pallas kernels, fused_body(): pl.pallas_call(partial(update_kernel, groups), out_shape=[jax.ShapeDtypeS...  2.37 us

profile of v1, /device:TPU:0, one launch (start us, length us, event | category | flops | bytes accessed | tf_op | source)
XLA Modules:
  0.0 92.2 jit_solution(3965904140372736838)
XLA Ops:
  0.7 89.0 %step.1 = (f32[8,16,128]{2,1,0:T(8,128)}, f32[8,40,128]{2,1,0:T(8,128)}, f32[64,128]{1,0:T(8,128)}, f32[8,128]{1,0:T(8,128)}) custom-call(bf16[2,32,256,128]{3,2,1,0:T(8,128)(2,1)} %refs_0_.1, s32[2]{0:T(128)} %refs_1_.1, s32[2,32,256]{2,1,0:T(8,128)} %refs_2_.1, f32[128,128]{1,0:T(8,128)} %refs_4_.1, f32[1,128]{1,0:T(1,128)} %bitcast.18, ...), custom_call_target="tpu_custom_call" | custom-call | tf_op jit(solution)/shard_map/step/pallas_call | solution.py:1025
  89.6 2.4 %update.1 = (f32[1,1]{1,0:T(1,128)}, f32[1,1]{1,0:T(1,128)}, f32[128,128]{1,0:T(8,128)}, f32[1,128]{1,0:T(1,128)}, f32[32,128]{1,0:T(8,128)}, /*index=5*/f32[128...) custom-call(f32[8,16,128]{2,1,0:T(8,128)} %get-tuple-element.50.refs, ...), custom_call_target="tpu_custom_call" | custom-call | tf_op jit(solution)/shard_map/update/pallas_call | solution.py:1042

commit v2 on v1

--- a/solution.py
+++ b/solution.py
@@ -306,21 +306,21 @@
 
 def step_kernel(groups, heads, *refs):
     (
-        pair, lengths, bins, head_w, bias_w, out_w, exp_w, red_w, dist_w, small,
+        pair_hbm, lengths, bins, head_w, bias_w, out_w, exp_w, red_w, dist_w, small,
         o_head, o_block, o_dist, o_small,
-        normed, tok, qkv, sig, expo, mixed, rinv,
-        wc, wt, we, wet, wr, wrt, wo, wot, wd, wdt, gain_col, dist_col,
+        pair, normed, tok, qkv, sig, expo, mixed, rinv,
+        wc, wt, we, wet, wr, wrt, wo, wot, wd, wdt, gain_col, dist_col, sel_a, sel_b,
         bias_f, bias_send, bias_all, bias_t, bins_low, bins_in, bins_own, bins_t,
         gated, gall, xhat, rstd, widened, hidden, slow, halves, pack_f, half_send, half_in, mirror,
-        dpre_s, first_s, dh_s, dsec_s, dtr_s, dout_s, dg_send, dg_in, g_out, g_red, g_exp, g_dist, loss_acc, dist_acc,
-        block_send, block_in, block_sum,
-        db_acc, ds_s, dm_s, dproj_s, db_send, db_in, g_head, g_bias, head_in, head_sum, small_own, small_in, card, card_in,
-        sem_bias_s, sem_bias_r, sem_bins_s, sem_bins_r, sem_w_s, sem_w_r,
-        sem_gat_s, sem_gat_r, sem_half_s, sem_half_r, sem_dg_s, sem_dg_r,
-        sem_blk_s, sem_blk_r, sem_gath_s, sem_gath_r, sem_db_s, sem_db_r,
-        sem_head_s, sem_head_r, sem_small_s, sem_small_r, sem_card_s, sem_card_r, sem_fin_s, sem_fin_r,
+        dpre_s, first_s, dh_s, dsec_s, dtr_s, dout_s, dg_send, dg_in,
+        g_out, g_red, g_exp, g_dist, loss_acc, dist_acc,
+        block_own, block_send, block_in, part_own, part_in, block_sum,
+        db_acc, ds_s, dm_s, dproj_s, db_send, db_in, g_head, g_bias, head_in, head_sum, card, card_in,
+        sem_pair, sem_bias, sem_bins, sem_w, sem_gat, sem_half, sem_dg,
+        sem_blk, sem_part, sem_gath, sem_db, sem_head, sem_card, sem_fin,
     ) = refs
     items, rows, length, chan = pair.shape
+    group_rows = 8
     width = out_w.shape[0]
     nbins = dist_w.shape[0]
     unit = exp_w.shape[1]
@@ -335,9 +335,9 @@
     def device(r, h):
         return {"res": r, "head": h}
 
-    def send(src, dst, ssem, rsem, r, h):
+    def send(src, dst, sem, r, h):
         return pltpu.make_async_remote_copy(
-            src_ref=src, dst_ref=dst, send_sem=ssem, recv_sem=rsem,
+            src_ref=src, dst_ref=dst, send_sem=sem.at[0], recv_sem=sem.at[1],
             device_id=device(r, h), device_id_type=pl.DeviceIdType.MESH,
         )
 
@@ -351,15 +351,21 @@
         d = lax.rem(me + o, total)
         return d, d // heads, lax.rem(d, heads)
 
-    def each(count, make, act):
+    def start(count, make):
         def one(o, carry):
-            act(make(o))
+            make(o).start()
             return carry
         lax.fori_loop(1, count, one, 0)
 
-    start = lambda c: c.start()
-    wait_in = lambda c: c.wait_recv()
-    wait_out = lambda c: c.wait_send()
+    def wait_in(ref, sem):
+        send(ref, ref, sem, res_peer(1), my_h).wait_recv()
+
+    def wait_out(ref, sem):
+        send(ref, ref, sem, res_peer(1), my_h).wait_send()
+
+    def load(item, t):
+        at = pl.ds(t * group_rows, group_rows)
+        return pltpu.make_async_copy(pair_hbm.at[item, at], pair.at[item, at], sem_pair.at[item, t])
 
     barrier = pltpu.get_barrier_semaphore()
 
@@ -370,35 +376,51 @@
 
     lax.fori_loop(1, total, greet, 0)
 
-    hw = head_w[...]
-    hw_low = hw.astype(LOW)
-    wc[0 : 4 * width] = jnp.transpose(hw).astype(LOW)
+    for item in range(items):
+        for t in range(rows // group_rows):
+            load(item, t).start()
+
     brow = bias_w[...].astype(LOW).astype(F32)
-    wc[4 * width :] = jnp.where(iota((16, chan), 0) == 0, brow, 0.0).astype(LOW)
-    src_col = iota((4 * width, 4 * width), 0)
-    dst_col = iota((4 * width, 4 * width), 1)
-    want = jnp.where(
-        dst_col < width, dst_col + width, jnp.where(dst_col < 3 * width, dst_col, -1)
-    )
-    wt[...] = dot(hw_low, (src_col == want).astype(F32).astype(LOW)).astype(LOW)
+    gain_one = small[0:chan].reshape(1, chan)
+    gain_two = small[chan : 2 * chan].reshape(1, chan)
     ident = eye(chan)
     ident_l = eye(length)
     center_by = (ident.astype(F32) - 1.0 / chan).astype(LOW)
-    gain_one = small[0:chan].reshape(1, chan)
-    gain_two = small[chan : 2 * chan].reshape(1, chan)
-    bins_row = jnp.concatenate(
-        [small[2 * chan : 2 * chan + nbins].reshape(1, nbins), jnp.zeros((1, chan - nbins), F32)], 1
-    )
-    gain_col[...] = jnp.transpose(jnp.broadcast_to(gain_two, (chan, chan)))
-    dist_col[...] = jnp.transpose(jnp.broadcast_to(bins_row, (chan, chan)))[:nbins]
-    we[:, pl.ds(pl.multiple_of(my_h * unit, unit), unit)] = exp_w[...].astype(LOW)
-    wr[pl.ds(pl.multiple_of(my_h * unit, unit), unit), :] = red_w[...].astype(LOW)
-    wo[pl.ds(pl.multiple_of(my_h * width, width), width), :] = out_w[...].astype(LOW)
-    wdt[...] = dist_w[...].astype(LOW)
-    wd[...] = dot(ident, wdt[...], NT).astype(LOW)
-    bins_low[...] = bins[...].astype(F32).astype(LOW)
-    bins_own[...] = bins[:, pl.ds(pl.multiple_of(my_h * own, own), own), :].astype(F32)
     one_lane = (iota((1, 4 * width), 1) >= 3 * width).astype(F32)
+
+    def prepare_first():
+        hw = head_w[...]
+        wc[0 : 4 * width] = jnp.transpose(hw).astype(LOW)
+        wc[4 * width :] = jnp.where(iota((16, chan), 0) == 0, brow, 0.0).astype(LOW)
+        src_col = iota((4 * width, 4 * width), 0)
+        dst_col = iota((4 * width, 4 * width), 1)
+        want = jnp.where(
+            dst_col < width, dst_col + width, jnp.where(dst_col < 3 * width, dst_col, -1)
+        )
+        wt[...] = dot(hw.astype(LOW), (src_col == want).astype(F32).astype(LOW)).astype(LOW)
+
+    def prepare_weights():
+        we[:, pl.ds(pl.multiple_of(my_h * unit, unit), unit)] = exp_w[...].astype(LOW)
+        wr[pl.ds(pl.multiple_of(my_h * unit, unit), unit), :] = red_w[...].astype(LOW)
+        wo[pl.ds(pl.multiple_of(my_h * width, width), width), :] = out_w[...].astype(LOW)
+
+    def prepare_rest():
+        bins_row = jnp.concatenate(
+            [small[2 * chan : 2 * chan + nbins].reshape(1, nbins), jnp.zeros((1, chan - nbins), F32)], 1
+        )
+        gain_col[...] = jnp.transpose(jnp.broadcast_to(gain_two, (chan, chan)))
+        dist_col[...] = jnp.transpose(jnp.broadcast_to(bins_row, (chan, chan)))[:nbins]
+        wdt[...] = dist_w[...].astype(LOW)
+        wd[...] = dot(ident, wdt[...], NT).astype(LOW)
+        bins_low[...] = bins[...].astype(F32).astype(LOW)
+        bins_own[...] = bins[:, pl.ds(pl.multiple_of(my_h * own, own), own), :].astype(F32)
+        sel_row = iota((total * half_own, length), 0)
+        sel_col = iota((total * half_own, length), 1)
+        sel_at = sel_row // half_own * own + lax.rem(sel_row, half_own)
+        sel_a[...] = (sel_col == sel_at).astype(F32).astype(LOW)
+        sel_b[...] = (sel_col == sel_at + half_own).astype(F32).astype(LOW)
+        for ref in (g_out, g_red, g_exp, g_dist, loss_acc, dist_acc, g_head, g_bias):
+            ref[...] = jnp.zeros_like(ref)
 
     def before(item):
         def norm(r):
@@ -415,6 +437,7 @@
             tok[item, r] = (dot(low, wt[...]) + one_lane).astype(LOW)
 
         def group(t, carry):
+            load(item, t).wait()
             for k in range(8 + 8):
                 if k < 8:
                     norm(t * 8 + k)
@@ -430,7 +453,7 @@
             return send(
                 bias_send.at[item],
                 bias_all.at[item, pl.ds(pl.multiple_of(my_r * rows, rows), rows), :],
-                sem_bias_s.at[item, o], sem_bias_r.at[item, o], res_peer(o), my_h,
+                sem_bias.at[item], res_peer(o), my_h,
             )
         return make
 
@@ -440,20 +463,20 @@
     def bins_copy(o):
         return send(
             bins_low.at[:, :, bins_block(res_peer(o))], bins_in.at[my_r],
-            sem_bins_s.at[o], sem_bins_r.at[o], res_peer(o), my_h,
+            sem_bins, res_peer(o), my_h,
         )
 
     def we_copy(o):
         at = (slice(None), pl.ds(pl.multiple_of(my_h * unit, unit), unit))
-        return send(we.at[at], we.at[at], sem_w_s.at[0, o], sem_w_r.at[0, o], my_r, head_peer(o))
+        return send(we.at[at], we.at[at], sem_w.at[0], my_r, head_peer(o))
 
     def wr_copy(o):
         at = pl.ds(pl.multiple_of(my_h * unit, unit), unit)
-        return send(wr.at[at], wr.at[at], sem_w_s.at[1, o], sem_w_r.at[1, o], my_r, head_peer(o))
+        return send(wr.at[at], wr.at[at], sem_w.at[1], my_r, head_peer(o))
 
     def wo_copy(o):
         at = pl.ds(pl.multiple_of(my_h * width, width), width)
-        return send(wo.at[at], wo.at[at], sem_w_s.at[2, o], sem_w_r.at[2, o], my_r, head_peer(o))
+        return send(wo.at[at], wo.at[at], sem_w.at[2], my_r, head_peer(o))
 
     def gated_copy(item):
         def make(o):
@@ -461,7 +484,7 @@
             return send(
                 gated.at[item, pl.ds(p * own, own)],
                 gall.at[item, :, pl.ds(pl.multiple_of(my_h * width, width), width), :],
-                sem_gat_s.at[item, o], sem_gat_r.at[item, o], my_r, p,
+                sem_gat.at[item], my_r, p,
             )
         return make
 
@@ -513,12 +536,6 @@
 
     def pair_of(ref, item, t):
         return jnp.concatenate([ref[item, t], ref[item, t + half_own]], 1)
-
-    sel_row = iota((total * half_own, length), 0)
-    sel_col = iota((total * half_own, length), 1)
-    sel_at = sel_row // half_own * own + lax.rem(sel_row, half_own)
-    sel_a = (sel_col == sel_at).astype(F32).astype(LOW)
-    sel_b = (sel_col == sel_at + half_own).astype(F32).astype(LOW)
 
     def forward(item):
         gc = jnp.concatenate([gain_col[...]] * (2 * length // chan), 1)
@@ -555,8 +572,8 @@
         def pack(t):
             for k in range(2):
                 part = halves[item, t + k * half_own].astype(LOW)
-                packed = dot(sel_a, jnp.concatenate([part, zero], 0), NT) + dot(
-                    sel_b, jnp.concatenate([zero, part], 0), NT
+                packed = dot(sel_a[...], jnp.concatenate([part, zero], 0), NT) + dot(
+                    sel_b[...], jnp.concatenate([zero, part], 0), NT
                 )
                 pack_f[pl.ds(t + k * half_own, total * half_own, own), :] = packed
 
@@ -569,7 +586,7 @@
             d, r, h = any_peer(o)
             return send(
                 half_send.at[item, d], half_in.at[item, me],
-                sem_half_s.at[item, o], sem_half_r.at[item, o], r, h,
+                sem_half.at[item], r, h,
             )
         return make
 
@@ -657,7 +674,7 @@
             p = head_peer(o)
             return send(
                 dg_send.at[item, p], dg_in.at[item, pl.ds(my_h * own, own)],
-                sem_dg_s.at[item, o], sem_dg_r.at[item, o], my_r, p,
+                sem_dg.at[item], my_r, p,
             )
         return make
 
@@ -709,7 +726,7 @@
             p = res_peer(o)
             return send(
                 db_send.at[item, pl.ds(pl.multiple_of(p * rows, rows), rows), :], db_in.at[item, my_r],
-                sem_db_s.at[item, o], sem_db_r.at[item, o], p, my_h,
+                sem_db.at[item], p, my_h,
             )
         return make
 
@@ -718,39 +735,58 @@
         for s in range(1, groups):
             db = db + db_in[item, s].astype(F32)
         db = db.astype(LOW).astype(F32)
-        at = iota((rows, length), 0)
-
-        def row(r, acc):
-            return acc + dot(jnp.where(at == r, db, 0.0).astype(LOW), normed[item, r])
-        acc = lax.fori_loop(0, rows, row, jnp.zeros((rows, chan), F32), unroll=4)
+        at = iota((8, length), 0)
+        acc = jnp.zeros((8, chan), F32)
+        for g in range(rows // 8):
+            part = db[8 * g : 8 * g + 8]
+            spread = jnp.concatenate([jnp.where(at == q, part, 0.0) for q in range(8)], 1)
+            acc = acc + dot(
+                spread.astype(LOW), normed[item, 8 * g : 8 * g + 8].reshape(8 * length, chan)
+            )
         g_bias[...] += jnp.sum(acc, 0, keepdims=True)
 
+    ru, rw, rb = unit // groups, width // groups, nbins // total
+    piece = 2 * ru + 8
+
     def block_copy(o):
-        d, r, h = any_peer(o)
-        return send(block_send.at[d], block_in.at[me], sem_blk_s.at[o], sem_blk_r.at[o], r, h)
+        p = head_peer(o)
+        return send(block_send.at[p], block_in.at[my_h], sem_blk, my_r, p)
+
+    def part_copy(o):
+        p = res_peer(o)
+        return send(
+            part_own.at[pl.ds(pl.multiple_of(p * piece, 8), piece), :], part_in.at[my_r], sem_part, p, my_h
+        )
 
     def gather_copy(o):
-        return send(block_sum, o_block.at[my_r], sem_gath_s.at[o], sem_gath_r.at[o], res_peer(o), my_h)
-
-    ru, rw, rb = unit // groups, width // groups, nbins // total
+        return send(block_sum, o_block.at[my_r], sem_gath, res_peer(o), my_h)
 
     def block_make():
-        for r in range(groups):
-            for h in range(heads):
-                d = r * heads + h
+        for h in range(heads):
+            for r in range(groups):
+                base = r * piece
                 at = h * unit + r * ru
-                block_send[d, 0:ru] = g_red[at : at + ru]
-                block_send[d, ru : 2 * ru] = g_exp[at : at + ru]
+                block_own[h, base : base + ru] = g_red[at : at + ru]
+                block_own[h, base + ru : base + 2 * ru] = g_exp[at : at + ru]
                 at = h * width + r * rw
-                block_send[d, 2 * ru : 2 * ru + rw] = g_out[at : at + rw]
-                block_send[d, 2 * ru + rw : 2 * ru + rw + rb] = g_dist[d * rb : (d + 1) * rb]
-                block_send[d, 2 * ru + rw + rb :] = jnp.zeros((8 - rw - rb, chan), F32)
-        block_in[me] = block_send[me]
+                base += 2 * ru
+                block_own[h, base : base + rw] = g_out[at : at + rw]
+                at = (r * heads + h) * rb
+                block_own[h, base + rw : base + rw + rb] = g_dist[at : at + rb]
+                block_own[h, base + rw + rb : base + 8] = jnp.zeros((8 - rw - rb, chan), F32)
+            block_send[h] = block_own[h].astype(LOW)
+
+    def part_make():
+        acc = block_own[my_h]
+        for o in range(1, heads):
+            acc = acc + block_in[head_peer(o)].astype(F32)
+        part_own[...] = acc
+        part_in[my_r] = part_own[pl.ds(pl.multiple_of(my_r * piece, 8), piece), :]
 
     def block_add():
-        acc = block_in[0]
-        for d in range(1, total):
-            acc = acc + block_in[d]
+        acc = part_in[0]
+        for r in range(1, groups):
+            acc = acc + part_in[r]
         block_sum[...] = acc
         o_block[my_r] = acc
 
@@ -758,72 +794,97 @@
         p = res_peer(o)
         return send(
             g_head.at[pl.ds(pl.multiple_of(p * (4 * width // groups), 4 * width // groups), 4 * width // groups), :],
-            head_in.at[my_r], sem_head_s.at[o], sem_head_r.at[o], p, my_h,
-        )
-
-    def small_copy(o):
-        return send(small_own, small_in.at[my_r], sem_small_s.at[o], sem_small_r.at[o], res_peer(o), my_h)
+            head_in.at[my_r], sem_head, p, my_h,
+        )
 
     def card_copy(o):
         d, r, h = any_peer(o)
-        return send(card, card_in.at[me], sem_card_s.at[o], sem_card_r.at[o], r, h)
+        return send(card, card_in.at[me], sem_card, r, h)
 
     def fin_copy(o):
-        return send(head_sum, o_head.at[my_r], sem_fin_s.at[o], sem_fin_r.at[o], res_peer(o), my_h)
-
-    for ref in (g_out, g_red, g_exp, g_dist, loss_acc, dist_acc, g_head, g_bias):
-        ref[...] = jnp.zeros_like(ref)
+        return send(head_sum, o_head.at[my_r], sem_fin, res_peer(o), my_h)
+
+    all_but = lambda ref, item, count: ref.at[item, pl.ds(0, count)]
+    bias_part = lambda item: all_but(bias_all, item, (groups - 1) * rows)
+    gat_part = lambda item: all_but(gated, item, (heads - 1) * own)
+    dg_part = lambda item: all_but(dg_in, item, (heads - 1) * own)
+    half_part = lambda item: all_but(half_in, item, total - 1)
+    db_part = lambda item: all_but(db_in, item, groups - 1)
+    bins_part = bins_in.at[pl.ds(0, groups - 1)]
+    w_parts = (
+        we.at[:, pl.ds(0, (heads - 1) * unit)], wr.at[pl.ds(0, (heads - 1) * unit)],
+        wo.at[pl.ds(0, (heads - 1) * width)],
+    )
+    blk_part = block_in.at[pl.ds(0, heads - 1)]
+    part_part = part_in.at[pl.ds(0, groups - 1)]
+    gath_part = o_block.at[pl.ds(0, groups - 1)]
+    head_part = head_in.at[pl.ds(0, groups - 1)]
+    fin_part = o_head.at[pl.ds(0, groups - 1)]
+    card_part = card_in.at[pl.ds(0, total - 1)]
+
+    prepare_first()
     before(0)
     pl.semaphore_wait(barrier, total - 1)
-    each(groups, bias_copy(0), start)
+    start(groups, bias_copy(0))
+    prepare_weights()
     for make in (we_copy, wr_copy, wo_copy):
-        each(heads, make, start)
+        start(heads, make)
     for item in range(1, items):
         before(item)
-        each(groups, bias_copy(item), start)
-    each(groups, bins_copy, start)
+        start(groups, bias_copy(item))
+    prepare_rest()
+    start(groups, bins_copy)
     bins_in[my_r] = bins_low[:, :, bins_block(my_r)]
     for item in range(items):
-        each(groups, bias_copy(item), wait_in)
+        wait_in(bias_part(item), sem_bias.at[item])
         attend(item)
-    for make in (we_copy, wr_copy, wo_copy):
-        each(heads, make, wait_in)
+    for k in range(3):
+        wait_in(w_parts[k], sem_w.at[k])
     for b in range(heads):
         at = slice(b * unit, (b + 1) * unit)
         wet[at] = dot(ident, we[:, at], NT).astype(LOW)
         wrt[:, at] = dot(ident, wr[at], NT).astype(LOW)
     wot[...] = dot(ident, wo[...], NT).astype(LOW)
     for item in range(items):
-        each(heads, gated_copy(item), wait_in)
+        wait_in(gat_part(item), sem_gat.at[item])
         forward(item)
-        each(total, half_copy(item), start)
-    each(groups, bins_copy, wait_in)
+        start(total, half_copy(item))
+    wait_in(bins_part, sem_bins)
     lane = my_r * rows + my_h * own - (my_r * rows) // 128 * 128
     pick = (iota((16, 128), 1) == iota((16, 128), 0) + lane).astype(F32).astype(LOW)
     for item in range(items):
         bins_t[item] = dot(pick, bins_in[:, item].reshape(groups * rows, 128), NT)
     for item in range(items):
-        each(total, half_copy(item), wait_in)
+        wait_in(half_part(item), sem_half.at[item])
         backward(item)
-        each(heads, dg_copy(item), start)
+        start(heads, dg_copy(item))
     block_make()
-    each(total, block_copy, start)
+    start(heads, block_copy)
     for item in range(items):
-        each(heads, dg_copy(item), wait_in)
+        wait_in(dg_part(item), sem_dg.at[item])
         attend_back(item)
-        each(groups, db_copy(item), start)
+        start(groups, db_copy(item))
         if item == 0:
-            each(total, block_copy, wait_in)
-            block_add()
-            each(groups, gather_copy, start)
-    each(groups, head_copy, start)
+            wait_in(blk_part, sem_blk)
+            part_make()
+            start(groups, part_copy)
+    start(groups, head_copy)
     sh = 4 * width // groups
     head_in[my_r] = g_head[pl.ds(pl.multiple_of(my_r * sh, sh), sh), :]
-    for item in range(items):
-        each(groups, db_copy(item), wait_in)
+    wait_in(part_part, sem_part)
+    block_add()
+    start(groups, gather_copy)
+    for item in range(items - 1):
+        wait_in(db_part(item), sem_db.at[item])
         bias_back(item)
-    gb = g_bias[...]
-    up_one = jnp.sum(wc[0 : 4 * width].astype(F32) * g_head[...], 0, keepdims=True) + brow * gb
+    wait_in(head_part, sem_head)
+    acc = head_in[0]
+    for r in range(1, groups):
+        acc = acc + head_in[r]
+    head_sum[...] = acc
+    o_head[my_r] = acc
+    start(groups, fin_copy)
+    up_one = jnp.sum(wc[0 : 4 * width].astype(F32) * g_head[...], 0, keepdims=True)
     up_two = jnp.sum(wet[...].astype(F32) * g_exp[...], 0, keepdims=True)
     dacc = dist_acc[:, 0:chan]
     lacc = loss_acc[:, 0:chan]
@@ -831,67 +892,57 @@
         dacc = dacc + dist_acc[:, k * chan : (k + 1) * chan]
         lacc = lacc + loss_acc[:, k * chan : (k + 1) * chan]
     dacc = jnp.transpose(jnp.concatenate([dacc, jnp.zeros((chan - nbins, chan), F32)], 0))
-    small_own[0:1] = gb
-    small_own[1:2] = up_one / gain_one
-    small_own[2:3] = up_two / gain_two
-    small_own[3:4] = jnp.sum(dacc, 0, keepdims=True)
-    small_own[4:5] = lacc
-    small_own[5:8] = jnp.zeros((3, chan), F32)
-    small_in[my_r] = small_own[...]
-    each(groups, small_copy, start)
-    each(groups, head_copy, wait_in)
-    acc = head_in[0]
-    for s in range(1, groups):
-        acc = acc + head_in[s]
-    head_sum[...] = acc
-    o_head[my_r] = acc
-    each(groups, fin_copy, start)
-    each(groups, small_copy, wait_in)
-    tiny = small_in[0]
-    for s in range(1, groups):
-        tiny = tiny + small_in[s]
     blocks = block_sum[...]
-    squares = jnp.sum(acc * acc, 0, keepdims=True) + jnp.sum(blocks * blocks, 0, keepdims=True)
-    card[...] = tiny
-    card[5:6] = squares
+    card[2:3] = up_two / gain_two
+    card[3:4] = jnp.sum(dacc, 0, keepdims=True)
+    card[4:5] = lacc
+    card[5:6] = jnp.sum(acc * acc, 0, keepdims=True) + jnp.sum(blocks * blocks, 0, keepdims=True)
     card[6:8] = blocks[2 * ru + rw : 2 * ru + rw + rb]
+    wait_in(db_part(items - 1), sem_db.at[items - 1])
+    bias_back(items - 1)
+    gb = g_bias[...]
+    card[0:1] = gb
+    card[1:2] = (up_one + brow * gb) / gain_one
     card_in[me] = card[...]
-    each(total, card_copy, start)
-    each(total, card_copy, wait_in)
-    every = card_in[0]
-    for d in range(1, total):
-        every = every + card_in[d]
-    mine = [card_in[my_r * heads + h] for h in range(heads)]
-    summed = mine[0]
-    bias_sq = mine[0] * mine[0]
-    for h in range(1, heads):
-        summed = summed + mine[h]
-        bias_sq = bias_sq + mine[h] * mine[h]
+    start(total, card_copy)
+    wait_in(card_part, sem_card)
+    by_head = [card_in[h] for h in range(heads)]
+    for r in range(1, groups):
+        by_head = [a + card_in[r * heads + h] for h, a in enumerate(by_head)]
+    every = by_head[0]
+    bias_sq = by_head[0] * by_head[0]
+    for a in by_head[1:]:
+        every = every + a
+        bias_sq = bias_sq + a * a
     norm_sq = every[5:6] + bias_sq[0:1]
     for k in (1, 2, 3):
-        norm_sq = norm_sq + summed[k : k + 1] * summed[k : k + 1]
+        norm_sq = norm_sq + every[k : k + 1] * every[k : k + 1]
     norm = jnp.sqrt(jnp.sum(norm_sq, -1, keepdims=True))
-    o_small[...] = summed
-    o_small[0:1] = card[0:1]
-    o_small[4:5] = jnp.broadcast_to(jnp.sum(summed[4:5], -1, keepdims=True), (1, chan))
+    o_small[...] = every
+    mine = card_in[my_h]
+    for r in range(1, groups):
+        mine = mine + card_in[r * heads + my_h]
+    o_small[0:1] = mine[0:1]
+    o_small[4:5] = jnp.broadcast_to(jnp.sum(every[4:5], -1, keepdims=True), (1, chan))
     o_small[5:6] = jnp.broadcast_to(norm, (1, chan))
     o_small[6:7] = jnp.broadcast_to(CLIP / jnp.maximum(norm, CLIP), (1, chan))
     for d in range(total):
         o_dist[d * rb : (d + 1) * rb] = card_in[d, 6 : 6 + rb]
-    each(groups, gather_copy, wait_in)
-    each(groups, fin_copy, wait_in)
+    wait_in(gath_part, sem_gath)
+    wait_in(fin_part, sem_fin)
     for item in range(items):
-        each(groups, bias_copy(item), wait_out)
-        each(heads, gated_copy(item), wait_out)
-        each(total, half_copy(item), wait_out)
-        each(heads, dg_copy(item), wait_out)
-        each(groups, db_copy(item), wait_out)
-    for make in (we_copy, wr_copy, wo_copy):
-        each(heads, make, wait_out)
-    for make in (bins_copy, gather_copy, head_copy, small_copy, fin_copy):
-        each(groups, make, wait_out)
-    for make in (block_copy, card_copy):
-        each(total, make, wait_out)
+        wait_out(bias_part(item), sem_bias.at[item])
+        wait_out(gat_part(item), sem_gat.at[item])
+        wait_out(half_part(item), sem_half.at[item])
+        wait_out(dg_part(item), sem_dg.at[item])
+        wait_out(db_part(item), sem_db.at[item])
+    for k in range(3):
+        wait_out(w_parts[k], sem_w.at[k])
+    for ref, sem in (
+        (bins_part, sem_bins), (blk_part, sem_blk), (part_part, sem_part), (gath_part, sem_gath),
+        (head_part, sem_head), (fin_part, sem_fin), (card_part, sem_card),
+    ):
+        wait_out(ref, sem)
 
 
 def update_kernel(groups, *refs):
@@ -947,6 +998,7 @@
     dma = pltpu.SemaphoreType.DMA
     scratch = [
         V((items, rows, length, chan), LOW),
+        V((items, rows, length, chan), LOW),
         V((items, rows, length, 4 * width), LOW),
         V((items, rows, 3 * width, length), LOW),
         V((items, rows, width, length), F32),
@@ -965,6 +1017,8 @@
         V((nbins, chan), LOW),
         V((chan, chan), F32),
         V((nbins, chan), F32),
+        V((total * half_own, length), LOW),
+        V((total * half_own, length), LOW),
         V((rows, length), F32),
         V((items, rows, length), LOW),
         V((items, length, length), LOW),
@@ -999,8 +1053,11 @@
         V((nbins, chan), F32),
         V((1, length), F32),
         V((nbins, length), F32),
-        V((total, block_rows, chan), F32),
-        V((total, block_rows, chan), F32),
+        V((heads, groups * block_rows, chan), F32),
+        V((heads, groups * block_rows, chan), LOW),
+        V((heads, groups * block_rows, chan), LOW),
+        V((groups * block_rows, chan), F32),
+        V((groups, block_rows, chan), F32),
         V((block_rows, chan), F32),
         V((length, length), F32),
         V((8, length, length), LOW),
@@ -1013,15 +1070,24 @@
         V((groups, sh, chan), F32),
         V((sh, chan), F32),
         V((8, chan), F32),
-        V((groups, 8, chan), F32),
-        V((8, chan), F32),
         V((total, 8, chan), F32),
     ]
-    for shape in (
-        (items, groups), (groups,), (3, heads), (items, heads), (items, total), (items, heads),
-        (total,), (groups,), (items, groups), (groups,), (groups,), (total,), (groups,),
-    ):
-        scratch += [dma(shape), dma(shape)]
+    scratch += [
+        dma((items, rows // 8)),
+        dma((items, 2)),
+        dma((2,)),
+        dma((3, 2)),
+        dma((items, 2)),
+        dma((items, 2)),
+        dma((items, 2)),
+        dma((2,)),
+        dma((2,)),
+        dma((2,)),
+        dma((items, 2)),
+        dma((2,)),
+        dma((2,)),
+        dma((2,)),
+    ]
     grads = pl.pallas_call(
         partial(step_kernel, groups, heads),
         out_shape=[
@@ -1030,7 +1096,7 @@
             jax.ShapeDtypeStruct((nbins, chan), F32),
             jax.ShapeDtypeStruct((8, chan), F32),
         ],
-        in_specs=[vmem, pl.BlockSpec(memory_space=pltpu.SMEM)] + [vmem] * 8,
+        in_specs=[pl.BlockSpec(memory_space=pl.ANY), pl.BlockSpec(memory_space=pltpu.SMEM)] + [vmem] * 8,
         out_specs=[vmem] * 4,
         scratch_shapes=scratch,
         compiler_params=pltpu.CompilerParams(

time: 92.3 us -> 76.4 us (0.83)
  Pallas kernels: 91.3 us -> 75.4 us
    pallas_call x1, Pallas kernels: 89 us -> 73 us  [fused_body(): pl.pallas_call(partial(step_kernel, groups, heads), out_shape=[jax.ShapeD...]
where the time goes in v2:
time: 76.4 us; the launch traced here: 76.2 us
  Pallas kernels  75.4 us (99%)
  between operations  0.82 us (1%)
    pallas_call x1, Pallas kernels, fused_body(): pl.pallas_call(partial(step_kernel, groups, heads), out_shape=[jax.ShapeD...  73 us
    pallas_call x1, Pallas kernels, fused_body(): pl.pallas_call(partial(update_kernel, groups), out_shape=[jax.ShapeDtypeS...  2.37 us

profile of v2, /device:TPU:0, one launch (start us, length us, event | category | flops | bytes accessed | tf_op | source)
XLA Modules:
  0.0 76.2 jit_solution(9849697146436623759)
XLA Ops:
  0.7 73.0 %step.1 = (f32[8,16,128]{2,1,0:T(8,128)}, f32[8,40,128]{2,1,0:T(8,128)}, f32[64,128]{1,0:T(8,128)}, f32[8,128]{1,0:T(8,128)}) custom-call(bf16[2,32,256,128]{3,2,1,0:T(8,128)(2,1)} %refs_0_.1, s32[2]{0:T(128)} %refs_1_.1, s32[2,32,256]{2,1,0:T(8,128)} %refs_2_.1, f32[128,128]{1,0:T(8,128)} %refs_4_.1, f32[1,128]{1,0:T(1,128)} %bitcast.18, ...), custom_call_target="tpu_custom_call" | custom-call | tf_op jit(solution)/shard_map/step/pallas_call | solution.py:1091
  73.7 2.4 %update.1 = (f32[1,1]{1,0:T(1,128)}, f32[1,1]{1,0:T(1,128)}, f32[128,128]{1,0:T(8,128)}, f32[1,128]{1,0:T(1,128)}, f32[32,128]{1,0:T(8,128)}, /*index=5*/f32[128...) custom-call(f32[8,16,128]{2,1,0:T(8,128)} %get-tuple-element.50.refs, ...), custom_call_target="tpu_custom_call" | custom-call | tf_op jit(solution)/shard_map/update/pallas_call | solution.py:1108

commit v3 on v2

--- a/solution.py
+++ b/solution.py
@@ -314,10 +314,10 @@
         gated, gall, xhat, rstd, widened, hidden, slow, halves, pack_f, half_send, half_in, mirror,
         dpre_s, first_s, dh_s, dsec_s, dtr_s, dout_s, dg_send, dg_in,
         g_out, g_red, g_exp, g_dist, loss_acc, dist_acc,
-        block_own, block_send, block_in, part_own, part_in, block_sum,
-        db_acc, ds_s, dm_s, dproj_s, db_send, db_in, g_head, g_bias, head_in, head_sum, card, card_in,
+        block_own, core_send, core_in, core_sum, block_send, block_in, part_own, part_in, block_sum, block_low,
+        db_acc, ds_s, dm_s, dproj_s, db_send, db_in, g_head, g_bias, head_in, head_low, card, card_in,
         sem_pair, sem_bias, sem_bins, sem_w, sem_gat, sem_half, sem_dg,
-        sem_blk, sem_part, sem_gath, sem_db, sem_head, sem_card, sem_fin,
+        sem_core, sem_blk, sem_part, sem_gath, sem_db, sem_head, sem_card, sem_fin,
     ) = refs
     items, rows, length, chan = pair.shape
     group_rows = 8
@@ -345,7 +345,8 @@
         return lax.rem(my_r + o, groups)
 
     def head_peer(o):
-        return lax.rem(my_h + o, heads)
+        flip, cross = o // 2 % 2, (o + 1) // 2 % 2
+        return lax.rem(my_h + flip * (1 - 2 * lax.rem(my_h, 2)) + 2 * cross, heads)
 
     def any_peer(o):
         d = lax.rem(me + o, total)
@@ -419,7 +420,7 @@
         sel_at = sel_row // half_own * own + lax.rem(sel_row, half_own)
         sel_a[...] = (sel_col == sel_at).astype(F32).astype(LOW)
         sel_b[...] = (sel_col == sel_at + half_own).astype(F32).astype(LOW)
-        for ref in (g_out, g_red, g_exp, g_dist, loss_acc, dist_acc, g_head, g_bias):
+        for ref in (g_out, g_red, g_exp, g_dist, loss_acc, dist_acc, g_head, g_bias, db_acc):
             ref[...] = jnp.zeros_like(ref)
 
     def before(item):
@@ -674,12 +675,11 @@
             p = head_peer(o)
             return send(
                 dg_send.at[item, p], dg_in.at[item, pl.ds(my_h * own, own)],
-                sem_dg.at[item], my_r, p,
+                sem_dg.at[item, o // (heads - 1)], my_r, p,
             )
         return make
 
-    def attend_back(item):
-        db_acc[...] = jnp.zeros_like(db_acc)
+    def attend_back(item, first_o, last_o):
         tail_row = iota((16, length), 0)
 
         def first(r, k, tot):
@@ -697,7 +697,7 @@
             dm_s[k] = dm
             dproj_s[3 * width :, k * length : (k + 1) * length] = (dg * m * s * (1.0 - s)).astype(LOW)
             ds = expo[item, r].astype(F32) * dot(tok[item, r], rhs)
-            db_acc[...] += ds
+            db_acc[item] += ds
             ds_s[k] = ds.astype(LOW)
             return None
 
@@ -708,7 +708,8 @@
             dproj_s[width : 2 * width, at] = (dot(qkv[item, r, 0:width], ds, NT) * scale).astype(LOW)
             dproj_s[2 * width : 3 * width, at] = dot(dm_s[k], expo[item, r], NT).astype(LOW)
 
-        def group(t, carry):
+        def group(o, carry):
+            t = head_peer(o)
             tot = None
             for k in range(8 + 4):
                 if k < 8:
@@ -717,8 +718,10 @@
                     second(t * 8 + k - 4, k - 4)
             g_head[...] += dot(dproj_s[...], normed[item, pl.ds(t * 8, 8)].reshape(8 * length, chan))
             return carry
-        lax.fori_loop(0, rows // 8, group, 0)
-        db_send[item] = dot(ident_l, db_acc[...].astype(LOW), NT).astype(LOW)
+        lax.fori_loop(first_o, last_o, group, 0)
+
+    def pair_bias_back(item):
+        db_send[item] = dot(ident_l, db_acc[item].astype(LOW), NT).astype(LOW)
         db_in[item, my_r] = db_send[item, pl.ds(pl.multiple_of(my_r * rows, rows), rows), :]
 
     def db_copy(item):
@@ -748,47 +751,54 @@
     ru, rw, rb = unit // groups, width // groups, nbins // total
     piece = 2 * ru + 8
 
+    side, mate = my_h // 2, lax.rem(my_h, 2)
+
+    def core_copy():
+        return send(core_send, core_in, sem_core, my_r, head_peer(heads - 1))
+
     def block_copy(o):
-        p = head_peer(o)
-        return send(block_send.at[p], block_in.at[my_h], sem_blk, my_r, p)
-
-    def part_copy(o):
         p = res_peer(o)
-        return send(
-            part_own.at[pl.ds(pl.multiple_of(p * piece, 8), piece), :], part_in.at[my_r], sem_part, p, my_h
-        )
+        return send(block_send.at[p], block_in.at[my_r], sem_blk, p, my_h)
+
+    def part_copy():
+        at = pl.ds(pl.multiple_of((1 - side) * piece, 8), piece)
+        return send(part_own.at[at, :], part_in, sem_part, my_r, head_peer(1))
 
     def gather_copy(o):
-        return send(block_sum, o_block.at[my_r], sem_gath, res_peer(o), my_h)
+        return send(block_low, o_block.at[my_r], sem_gath, res_peer(o), my_h)
 
     def block_make():
-        for h in range(heads):
-            for r in range(groups):
-                base = r * piece
+        for r in range(groups):
+            for h in range(heads):
+                c, base = h % 2, h // 2 * piece
                 at = h * unit + r * ru
-                block_own[h, base : base + ru] = g_red[at : at + ru]
-                block_own[h, base + ru : base + 2 * ru] = g_exp[at : at + ru]
+                block_own[c, r, base : base + ru] = g_red[at : at + ru]
+                block_own[c, r, base + ru : base + 2 * ru] = g_exp[at : at + ru]
                 at = h * width + r * rw
                 base += 2 * ru
-                block_own[h, base : base + rw] = g_out[at : at + rw]
+                block_own[c, r, base : base + rw] = g_out[at : at + rw]
                 at = (r * heads + h) * rb
-                block_own[h, base + rw : base + rw + rb] = g_dist[at : at + rb]
-                block_own[h, base + rw + rb : base + 8] = jnp.zeros((8 - rw - rb, chan), F32)
-            block_send[h] = block_own[h].astype(LOW)
+                block_own[c, r, base + rw : base + rw + rb] = g_dist[at : at + rb]
+                block_own[c, r, base + rw + rb : base + 8] = jnp.zeros((8 - rw - rb, chan), F32)
+        core_send[...] = block_own[1 - mate].astype(LOW)
+
+    def core_add():
+        both = block_own[mate] + core_in[...].astype(F32)
+        core_sum[...] = both
+        block_send[...] = both.astype(LOW)
 
     def part_make():
-        acc = block_own[my_h]
-        for o in range(1, heads):
-            acc = acc + block_in[head_peer(o)].astype(F32)
+        acc = core_sum[my_r]
+        for o in range(1, groups):
+            acc = acc + block_in[res_peer(o)].astype(F32)
         part_own[...] = acc
-        part_in[my_r] = part_own[pl.ds(pl.multiple_of(my_r * piece, 8), piece), :]
 
     def block_add():
-        acc = part_in[0]
-        for r in range(1, groups):
-            acc = acc + part_in[r]
+        acc = part_own[pl.ds(pl.multiple_of(side * piece, 8), piece), :] + part_in[...]
         block_sum[...] = acc
-        o_block[my_r] = acc
+        low = jnp.concatenate([acc, jnp.zeros((8, chan), F32)], 0).astype(LOW)
+        block_low[...] = low
+        o_block[my_r] = low
 
     def head_copy(o):
         p = res_peer(o)
@@ -802,12 +812,13 @@
         return send(card, card_in.at[me], sem_card, r, h)
 
     def fin_copy(o):
-        return send(head_sum, o_head.at[my_r], sem_fin, res_peer(o), my_h)
+        return send(head_low, o_head.at[my_r], sem_fin, res_peer(o), my_h)
 
     all_but = lambda ref, item, count: ref.at[item, pl.ds(0, count)]
     bias_part = lambda item: all_but(bias_all, item, (groups - 1) * rows)
     gat_part = lambda item: all_but(gated, item, (heads - 1) * own)
-    dg_part = lambda item: all_but(dg_in, item, (heads - 1) * own)
+    dg_near = lambda item: all_but(dg_in, item, own)
+    dg_far = lambda item: all_but(dg_in, item, (heads - 2) * own)
     half_part = lambda item: all_but(half_in, item, total - 1)
     db_part = lambda item: all_but(db_in, item, groups - 1)
     bins_part = bins_in.at[pl.ds(0, groups - 1)]
@@ -815,8 +826,7 @@
         we.at[:, pl.ds(0, (heads - 1) * unit)], wr.at[pl.ds(0, (heads - 1) * unit)],
         wo.at[pl.ds(0, (heads - 1) * width)],
     )
-    blk_part = block_in.at[pl.ds(0, heads - 1)]
-    part_part = part_in.at[pl.ds(0, groups - 1)]
+    blk_part = block_in.at[pl.ds(0, groups - 1)]
     gath_part = o_block.at[pl.ds(0, groups - 1)]
     head_part = head_in.at[pl.ds(0, groups - 1)]
     fin_part = o_head.at[pl.ds(0, groups - 1)]
@@ -833,11 +843,12 @@
         before(item)
         start(groups, bias_copy(item))
     prepare_rest()
-    start(groups, bins_copy)
     bins_in[my_r] = bins_low[:, :, bins_block(my_r)]
     for item in range(items):
         wait_in(bias_part(item), sem_bias.at[item])
         attend(item)
+        if item == 0:
+            start(groups, bins_copy)
     for k in range(3):
         wait_in(w_parts[k], sem_w.at[k])
     for b in range(heads):
@@ -854,36 +865,43 @@
     pick = (iota((16, 128), 1) == iota((16, 128), 0) + lane).astype(F32).astype(LOW)
     for item in range(items):
         bins_t[item] = dot(pick, bins_in[:, item].reshape(groups * rows, 128), NT)
+    last = items - 1
     for item in range(items):
         wait_in(half_part(item), sem_half.at[item])
         backward(item)
         start(heads, dg_copy(item))
-    block_make()
-    start(heads, block_copy)
+        if item == last:
+            block_make()
+            core_copy().start()
+        wait_in(dg_near(item), sem_dg.at[item, 1])
+        attend_back(item, heads - 1, heads + 1)
+    wait_in(core_in, sem_core)
+    core_add()
+    start(groups, block_copy)
     for item in range(items):
-        wait_in(dg_part(item), sem_dg.at[item])
-        attend_back(item)
+        wait_in(dg_far(item), sem_dg.at[item, 0])
+        attend_back(item, 1, heads - 1)
+        pair_bias_back(item)
         start(groups, db_copy(item))
-        if item == 0:
-            wait_in(blk_part, sem_blk)
-            part_make()
-            start(groups, part_copy)
     start(groups, head_copy)
     sh = 4 * width // groups
     head_in[my_r] = g_head[pl.ds(pl.multiple_of(my_r * sh, sh), sh), :]
-    wait_in(part_part, sem_part)
-    block_add()
-    start(groups, gather_copy)
-    for item in range(items - 1):
+    wait_in(blk_part, sem_blk)
+    part_make()
+    part_copy().start()
+    for item in range(last):
         wait_in(db_part(item), sem_db.at[item])
         bias_back(item)
     wait_in(head_part, sem_head)
     acc = head_in[0]
     for r in range(1, groups):
         acc = acc + head_in[r]
-    head_sum[...] = acc
-    o_head[my_r] = acc
+    head_low[...] = acc.astype(LOW)
+    o_head[my_r] = acc.astype(LOW)
+    wait_in(part_in, sem_part)
+    block_add()
     start(groups, fin_copy)
+    start(groups, gather_copy)
     up_one = jnp.sum(wc[0 : 4 * width].astype(F32) * g_head[...], 0, keepdims=True)
     up_two = jnp.sum(wet[...].astype(F32) * g_exp[...], 0, keepdims=True)
     dacc = dist_acc[:, 0:chan]
@@ -898,8 +916,8 @@
     card[4:5] = lacc
     card[5:6] = jnp.sum(acc * acc, 0, keepdims=True) + jnp.sum(blocks * blocks, 0, keepdims=True)
     card[6:8] = blocks[2 * ru + rw : 2 * ru + rw + rb]
-    wait_in(db_part(items - 1), sem_db.at[items - 1])
-    bias_back(items - 1)
+    wait_in(db_part(last), sem_db.at[last])
+    bias_back(last)
     gb = g_bias[...]
     card[0:1] = gb
     card[1:2] = (up_one + brow * gb) / gain_one
@@ -934,12 +952,13 @@
         wait_out(bias_part(item), sem_bias.at[item])
         wait_out(gat_part(item), sem_gat.at[item])
         wait_out(half_part(item), sem_half.at[item])
-        wait_out(dg_part(item), sem_dg.at[item])
+        wait_out(dg_far(item), sem_dg.at[item, 0])
+        wait_out(dg_near(item), sem_dg.at[item, 1])
         wait_out(db_part(item), sem_db.at[item])
     for k in range(3):
         wait_out(w_parts[k], sem_w.at[k])
     for ref, sem in (
-        (bins_part, sem_bins), (blk_part, sem_blk), (part_part, sem_part), (gath_part, sem_gath),
+        (bins_part, sem_bins), (core_in, sem_core), (blk_part, sem_blk), (part_in, sem_part), (gath_part, sem_gath),
         (head_part, sem_head), (fin_part, sem_fin), (card_part, sem_card),
     ):
         wait_out(ref, sem)
@@ -966,12 +985,13 @@
         new_m[k][at] = velocity
         new_a[k][at] = average
 
-    put(0, jnp.transpose(g_head[...].reshape(weights[0].shape[1], chan)))
+    put(0, jnp.transpose(g_head[...].astype(F32).reshape(weights[0].shape[1], chan)))
     put(1, g_small[0:1])
-    put(3, jnp.transpose(g_block[:, ru : 2 * ru].reshape(unit, chan)))
-    put(4, g_block[:, 0:ru].reshape(unit, chan))
+    block = g_block[...].astype(F32)
+    put(3, jnp.transpose(block[:, ru : 2 * ru].reshape(unit, chan)))
+    put(4, block[:, 0:ru].reshape(unit, chan))
     for r in range(groups):
-        put(2, g_block[r, 2 * ru : 2 * ru + rw], (slice(r * rw, (r + 1) * rw), slice(None)))
+        put(2, block[r, 2 * ru : 2 * ru + rw], (slice(r * rw, (r + 1) * rw), slice(None)))
     nbins = weights[5].shape[0]
     put(5, g_dist[...])
     put(6, g_small[1], (slice(0, chan),))
@@ -1053,13 +1073,17 @@
         V((nbins, chan), F32),
         V((1, length), F32),
         V((nbins, length), F32),
-        V((heads, groups * block_rows, chan), F32),
-        V((heads, groups * block_rows, chan), LOW),
-        V((heads, groups * block_rows, chan), LOW),
-        V((groups * block_rows, chan), F32),
-        V((groups, block_rows, chan), F32),
+        V((2, groups, 2 * block_rows, chan), F32),
+        V((groups, 2 * block_rows, chan), LOW),
+        V((groups, 2 * block_rows, chan), LOW),
+        V((groups, 2 * block_rows, chan), F32),
+        V((groups, 2 * block_rows, chan), LOW),
+        V((groups, 2 * block_rows, chan), LOW),
+        V((2 * block_rows, chan), F32),
         V((block_rows, chan), F32),
-        V((length, length), F32),
+        V((block_rows, chan), F32),
+        V((block_rows + 8, chan), LOW),
+        V((items, length, length), F32),
         V((8, length, length), LOW),
         V((8, width, length), LOW),
         V((4 * width, 8 * length), LOW),
@@ -1068,7 +1092,7 @@
         V((4 * width, chan), F32),
         V((1, chan), F32),
         V((groups, sh, chan), F32),
-        V((sh, chan), F32),
+        V((sh, chan), LOW),
         V((8, chan), F32),
         V((total, 8, chan), F32),
     ]
@@ -1079,7 +1103,8 @@
         dma((3, 2)),
         dma((items, 2)),
         dma((items, 2)),
-        dma((items, 2)),
+        dma((items, 2, 2)),
+        dma((2,)),
         dma((2,)),
         dma((2,)),
         dma((2,)),
@@ -1091,8 +1116,8 @@
     grads = pl.pallas_call(
         partial(step_kernel, groups, heads),
         out_shape=[
-            jax.ShapeDtypeStruct((groups, sh, chan), F32),
-            jax.ShapeDtypeStruct((groups, block_rows, chan), F32),
+            jax.ShapeDtypeStruct((groups, sh, chan), LOW),
+            jax.ShapeDtypeStruct((groups, block_rows + 8, chan), LOW),
             jax.ShapeDtypeStruct((nbins, chan), F32),
             jax.ShapeDtypeStruct((8, chan), F32),
         ],
@@ -1123,7 +1148,7 @@
 def body(groups, heads, *args):
     items, rows, length, channels = args[0].shape
     own = rows // heads
-    if own == 8 and rows % 16 == 0 and length % 128 == 0:
+    if heads == 4 and own == 8 and rows % 16 == 0 and length % 128 == 0:
         return fused_body(groups, heads, *args)
     return general_body(*args)
 

time: 76.4 us -> 73.3 us (0.959)
  Pallas kernels: 75.4 us -> 72.3 us
    pallas_call x1, Pallas kernels: 73 us -> 69.9 us  [fused_body(): pl.pallas_call(partial(step_kernel, groups, heads), out_shape=[jax.ShapeD...]
where the time goes in v3:
time: 73.3 us; the launch traced here: 73.1 us
  Pallas kernels  72.3 us (99%)
  between operations  0.82 us (1%)
    pallas_call x1, Pallas kernels, fused_body(): pl.pallas_call(partial(step_kernel, groups, heads), out_shape=[jax.ShapeD...  69.9 us
    pallas_call x1, Pallas kernels, fused_body(): pl.pallas_call(partial(update_kernel, groups), out_shape=[jax.ShapeDtypeS...  2.38 us

profile of v3, /device:TPU:0, one launch (start us, length us, event | category | flops | bytes accessed | tf_op | source)
XLA Modules:
  0.0 73.1 jit_solution(6252089532686870998)
XLA Ops:
  0.7 69.9 %step.1 = (bf16[8,16,128]{2,1,0:T(8,128)(2,1)}, bf16[8,48,128]{2,1,0:T(8,128)(2,1)}, f32[64,128]{1,0:T(8,128)}, f32[8,128]{1,0:T(8,128)}) custom-call(bf16[2,32,256,128]{3,2,1,0:T(8,128)(2,1)} %refs_0_.1, s32[2]{0:T(128)} %refs_1_.1, s32[2,32,256]{2,1,0:T(8,128)} %refs_2_.1, f32[128,128]{1,0:T(8,128)} %refs_4_.1, f32[1,128]{1,0:T(1,128)} %bitcast.18, ...), custom_call_target="tpu_custom_call" | custom-call | tf_op jit(solution)/shard_map/step/pallas_call | solution.py:1116
  70.6 2.4 %update.1 = (f32[1,1]{1,0:T(1,128)}, f32[1,1]{1,0:T(1,128)}, f32[128,128]{1,0:T(8,128)}, f32[1,128]{1,0:T(1,128)}, f32[32,128]{1,0:T(8,128)}, /*index=5*/f32[128...) custom-call(bf16[8,16,128]{2,1,0:T(8,128)(2,1)} %get-tuple-element.5, ...), custom_call_target="tpu_custom_call" | custom-call | tf_op jit(solution)/shard_map/update/pallas_call | solution.py:1133

commit v4 on v3

--- a/solution.py
+++ b/solution.py
@@ -869,10 +869,11 @@
     for item in range(items):
         wait_in(half_part(item), sem_half.at[item])
         backward(item)
-        start(heads, dg_copy(item))
+        dg_copy(item)(heads - 1).start()
         if item == last:
             block_make()
             core_copy().start()
+        start(heads - 1, dg_copy(item))
         wait_in(dg_near(item), sem_dg.at[item, 1])
         attend_back(item, heads - 1, heads + 1)
     wait_in(core_in, sem_core)

time: 73.3 us -> 73.2 us (level)
  no operation moved by 1% of the time
where the time goes in v4:
time: 73.2 us; the launch traced here: 73 us
  Pallas kernels  72.1 us (98%)
  between operations  0.82 us (1%)
    pallas_call x1, Pallas kernels, fused_body(): pl.pallas_call(partial(step_kernel, groups, heads), out_shape=[jax.ShapeD...  69.8 us
    pallas_call x1, Pallas kernels, fused_body(): pl.pallas_call(partial(update_kernel, groups), out_shape=[jax.ShapeDtypeS...  2.38 us

profile of v4, /device:TPU:0, one launch (start us, length us, event | category | flops | bytes accessed | tf_op | source)
XLA Modules:
  0.0 73.0 jit_solution(1658850668636445186)
XLA Ops:
  0.7 69.8 %step.1 = (bf16[8,16,128]{2,1,0:T(8,128)(2,1)}, bf16[8,48,128]{2,1,0:T(8,128)(2,1)}, f32[64,128]{1,0:T(8,128)}, f32[8,128]{1,0:T(8,128)}) custom-call(bf16[2,32,256,128]{3,2,1,0:T(8,128)(2,1)} %refs_0_.1, s32[2]{0:T(128)} %refs_1_.1, s32[2,32,256]{2,1,0:T(8,128)} %refs_2_.1, f32[128,128]{1,0:T(8,128)} %refs_4_.1, f32[1,128]{1,0:T(1,128)} %bitcast.18, ...), custom_call_target="tpu_custom_call" | custom-call | tf_op jit(solution)/shard_map/step/pallas_call | solution.py:1117
  70.4 2.4 %update.1 = (f32[1,1]{1,0:T(1,128)}, f32[1,1]{1,0:T(1,128)}, f32[128,128]{1,0:T(8,128)}, f32[1,128]{1,0:T(1,128)}, f32[32,128]{1,0:T(8,128)}, /*index=5*/f32[128...) custom-call(bf16[8,16,128]{2,1,0:T(8,128)(2,1)} %get-tuple-element.5, ...), custom_call_target="tpu_custom_call" | custom-call | tf_op jit(solution)/shard_map/update/pallas_call | solution.py:1134
